TPU v7x, 512 devices: a whole 4x8x8 slice. The times are simulated.
512 devices in a mesh: src: 8 (over x, y_lo), gx: 16 (over z, core), gy: 4 (over y_hi).
Axes of the slice: x: 4, y: 8 (y_hi: 4, y_lo: 2; y = y_hi * 2 + y_lo), z: 8, core: 2. Of those that a mesh axis runs over, the one named last changes fastest.
Arguments:
- warm_potential: float32 [32, 64, 128, 128], P('src', 'gx', 'gy'), may hold values from -3 to 3
- warm_adjoint: float32 [32, 64, 128, 128], P('src', 'gx', 'gy'), may hold values from -3 to 3
- conductivity: float32 [64, 128, 128], P('gx', 'gy', 'src'), may hold values from 0.2 to 5
- electrodes: int32 [32, 2], replicated, may hold values from 0 to 8191
- receivers: int32 [128, 2], replicated, may hold values from 0 to 8191
- observed: float32 [32, 128], replicated, may hold values from -6 to 6
- source_order: int32 [32], replicated, may hold values from 0 to 31, each once
Outputs:
- gradient: float32 [64, 128, 128], P('gx', 'gy', 'src')
Inputs may be any that keep to these rules, and one draw needn't show every extreme that they name: `electrodes`: entries number surface cells as x * 128 + y. `receivers`: entries number surface cells as x * 128 + y.
All inputs are finite; a program needn't handle non-finite values.
Results may differ from a plain program's by a relative error of at most 0.0003.
Values sent between devices are 32-bit elements; how exact they have to be, the bound alone decides.
A program may use at most 64 MiB of HBM per device.

v0:
```python
import jax
import jax.numpy as jnp
from jax import lax
from jax.sharding import PartitionSpec as P

SWEEPS = 6
lowest = 0.05
highest = 2.0
centre = (highest + lowest) / 2.0
half_span = (highest - lowest) / 2.0
bound_ratio = centre / half_span
strength = 4.0


def padded_2(block, sides, width):
    for axis, dim in sides:
        count = lax.axis_size(axis)
        forward = [(i, i + 1) for i in range(count - 1)]
        backward = [(target, source) for source, target in forward]
        low = lax.ppermute(
            lax.slice_in_dim(block, block.shape[dim] - width, None, axis=dim), axis, forward
        )
        high = lax.ppermute(lax.slice_in_dim(block, 0, width, axis=dim), axis, backward)
        block = jnp.concatenate([low, block, high], axis=dim)
    return block


def harmonic(left, right):
    return jnp.where(right > 0, 2.0 * left * right / (left + right), left)


def slope_of(left, right):
    total = left + right
    return jnp.where(right > 0, 2.0 * right * right / (total * total), 1.0)


def neighbours(field, padded):
    widths = [(0, 0)] * (field.ndim - 1) + [(1, 1)]
    deeper = jnp.pad(field, widths)
    return (
        padded[..., :-2, 1:-1, :],
        padded[..., 2:, 1:-1, :],
        padded[..., 1:-1, :-2, :],
        padded[..., 1:-1, 2:, :],
        deeper[..., :-2],
        deeper[..., 2:],
    )


def face_tables(sigma, padded):
    others = neighbours(sigma, padded)
    depth = lax.broadcasted_iota(jnp.int32, sigma.shape, 2)
    surface = depth == 0
    coeffs = [harmonic(sigma, other) for other in others]
    slopes = [slope_of(sigma, other) for other in others]
    coeffs[4] = jnp.where(surface, 0.0, coeffs[4])
    slopes[4] = jnp.where(surface, 0.0, slopes[4])
    return (coeffs, slopes)


def apply_operator(field, padded, coeffs):
    others = neighbours(field, padded)
    total = coeffs[0] * (field - others[0])
    for index in range(1, 6):
        total = total + coeffs[index] * (field - others[index])
    return total


def solve(rhs, start, coeffs, inverse, pad_fn):
    residual = rhs - apply_operator(start, pad_fn(start), coeffs)
    update = inverse * residual / centre
    iterate = start
    factor = 1.0 / bound_ratio
    for sweep in range(SWEEPS):
        iterate = iterate + update
        residual = residual - apply_operator(update, pad_fn(update), coeffs)
        following = 1.0 / (2.0 * bound_ratio - factor)
        update = following * factor * update + 2.0 * following / half_span * (inverse * residual)
        factor = following
    return iterate + update


def gradient_term(potential, adjoint, padded_potential, padded_adjoint, slopes):
    near_potential = neighbours(potential, padded_potential)
    near_adjoint = neighbours(adjoint, padded_adjoint)
    total = slopes[0] * (potential - near_potential[0]) * (adjoint - near_adjoint[0])
    for index in range(1, 6):
        total = total + slopes[index] * (potential - near_potential[index]) * (
            adjoint - near_adjoint[index]
        )
    return total


def pad_joint(field):
    return padded_2(field, (("gx", 1), ("gy", 2)), 1)


def reduce_groups(partial_value, depth):
    summed = lax.psum(partial_value, "src")
    return lax.dynamic_slice_in_dim(summed, lax.axis_index("src") * depth, depth, 2)


def body(warm_potential, warm_adjoint, conductivity, electrodes, receivers, observed, source_order):
    panel = lax.all_gather(conductivity, "src", axis=2, tiled=True)
    group = lax.axis_index("src")
    slots = warm_potential.shape[0]
    width_x = panel.shape[0]
    ny_global = panel.shape[1] * lax.axis_size("gy")
    x_start = lax.axis_index("gx") * width_x
    potential_start, adjoint_start = (warm_potential, warm_adjoint)
    first_slot = group * slots
    y_start = lax.axis_index("gy") * panel.shape[1]
    width_y = panel.shape[1]
    depth_cells = panel.shape[2]
    coeffs, slopes = face_tables(panel, pad_joint(panel[None])[0])
    inverse = 1.0 / (coeffs[0] + coeffs[1] + coeffs[2] + coeffs[3] + coeffs[4] + coeffs[5])
    idents = lax.dynamic_slice_in_dim(source_order, first_slot, slots)
    pairs = jnp.take(electrodes, idents, axis=0)
    rows_observed = jnp.take(observed, idents, axis=0)

    def picker(cells):
        local_x = cells // ny_global - x_start
        local_y = cells % ny_global - y_start
        inside = (local_x >= 0) & (local_x < width_x) & (local_y >= 0) & (local_y < width_y)
        flat = local_x * width_y + local_y
        places = lax.broadcasted_iota(jnp.int32, (cells.shape[0], width_x * width_y), 1)
        return jnp.where((flat[:, None] == places) & inside[:, None], 1.0, 0.0).astype(jnp.float32)

    def on_surface(flat):
        field = jnp.zeros((slots, width_x, width_y, depth_cells), jnp.float32)
        return field.at[..., 0].set(flat.reshape(slots, width_x, width_y))

    source_surface = strength * (picker(pairs[:, 0]) - picker(pairs[:, 1]))
    potential = solve(on_surface(source_surface), potential_start, coeffs, inverse, pad_joint)
    pickup = picker(receivers[:, 0]) - picker(receivers[:, 1])
    top = potential[..., 0].reshape(slots, width_x * width_y)
    local_values = jnp.dot(
        top, pickup.T, precision=lax.Precision.HIGHEST, preferred_element_type=jnp.float32
    )
    predicted = lax.psum(local_values, ("gx", "gy"))
    misfit = predicted - rows_observed
    back = jnp.dot(
        misfit, pickup, precision=lax.Precision.HIGHEST, preferred_element_type=jnp.float32
    )
    adjoint = solve(on_surface(back), adjoint_start, coeffs, inverse, pad_joint)
    padded_both = pad_joint(jnp.concatenate([potential, adjoint], 0))
    term = gradient_term(potential, adjoint, padded_both[:slots], padded_both[slots:], slopes)
    partial_value = -jnp.sum(term, axis=0)
    return reduce_groups(partial_value, conductivity.shape[2])


def solution(mesh):
    in_specs = (
        P("src", "gx", "gy", None),
        P("src", "gx", "gy", None),
        P("gx", "gy", "src"),
        P(),
        P(),
        P(),
        P(),
    )
    out_specs = P("gx", "gy", "src")
    return jax.shard_map(body, mesh=mesh, in_specs=in_specs, out_specs=out_specs, check_vma=False)
```

profile of v0, /device:TPU:16, one launch (start us, length us, event | category | flops | bytes accessed | tf_op | source)
XLA Modules:
  0.0 592.4 jit_solution(16727907163246744626)
XLA Ops:
  7.3 29.0 %all_gather.3 = f32[4,32,128]{1,0,2:T(4,128)S(1)} all-gather(f32[4,32,16]{1,0,2:T(4,128)S(1)} %copy.69), channel_id=1, replica_groups=mesh['src'=8,'gx'=16,'gy'=4] {'src'}, dimensions={2}, use_global_device_ids=true | all-gather | bytes 73728 | tf_op jit(solution)/shard_map/all_gather | solution.py:104
  36.5 1.3 collective-permute-start.1
  37.8 3.0 collective-permute-start
  40.9 3.9 collective-permute-start.4
  50.0 5.4 collective-permute-start.3
  55.4 2.6 collective-permute-start.2
  58.0 21.9 %collective-permute-done.3 = f32[1,6,1,128]{2,1,3,0:T(8,128)S(1)} collective-permute-done((f32[1,6,1,128]{2,1,3,0:T(8,128)S(1)}, f32[1,6,1,128]{2,1,3,0:T(8,128)S(1)}, u32[]{:S(2)}, u32[]{:S(2)}) %collective-permute-start.3) | collective-permute-done | bytes 3104 | tf_op jit(solution)/shard_map/ppermute | solution.py:23
  80.5 1.7 fusion.293
  82.3 2.3 collective-permute-start.7
  84.7 5.6 collective-permute-start.6
  90.3 2.0 add_divide_fusion
  96.5 3.0 collective-permute-start.8
  100.5 1.9 collective-permute-start.11
  102.4 6.0 %collective-permute-start.10 = (f32[4,6,1,128]{3,2,1,0:T(1,128)S(1)}, f32[4,6,1,128]{3,2,1,0:T(1,128)S(1)}, u32[]{:S(2)}, u32[]{:S(2)}) collective-permute-start(f32[4,6,1,128]{3,2,1,0:T(1,128)S(1)} %get-tuple-element.118), channel_id=1, source_target_pairs={{0,1},{1,2},{2,3},{4,5},{5,6},{6,7},{8,9},{9,10},{10,11},{12,13},{... | collective-permute-start | bytes 36872 | tf_op jit(solution)/shard_map/ppermute | solution.py:20
  108.5 1.4 collective-permute-done.10
  111.4 5.8 collective-permute-start.12
  118.2 1.9 collective-permute-start.15
  120.1 6.0 %collective-permute-start.14 = (f32[4,6,1,128]{3,2,1,0:T(1,128)S(1)}, f32[4,6,1,128]{3,2,1,0:T(1,128)S(1)}, u32[]{:S(2)}, u32[]{:S(2)}) collective-permute-start(f32[4,6,1,128]{3,2,1,0:T(1,128)S(1)} %get-tuple-element.116), channel_id=1, source_target_pairs={{0,1},{1,2},{2,3},{4,5},{5,6},{6,7},{8,9},{9,10},{10,11},{12,13},{... | collective-permute-start | bytes 36872 | tf_op jit(solution)/shard_map/ppermute | solution.py:20
  126.2 1.4 collective-permute-done.14
  127.8 1.4 collective-permute-start.17
  129.3 5.9 collective-permute-start.16
  136.1 1.9 collective-permute-start.19
  138.0 6.0 %collective-permute-start.18 = (f32[4,6,1,128]{3,2,1,0:T(1,128)S(1)}, f32[4,6,1,128]{3,2,1,0:T(1,128)S(1)}, u32[]{:S(2)}, u32[]{:S(2)}) collective-permute-start(f32[4,6,1,128]{3,2,1,0:T(1,128)S(1)} %get-tuple-element.114), channel_id=1, source_target_pairs={{0,1},{1,2},{2,3},{4,5},{5,6},{6,7},{8,9},{9,10},{10,11},{12,13},{... | collective-permute-start | bytes 36872 | tf_op jit(solution)/shard_map/ppermute | solution.py:20
  144.7 5.5 collective-permute-start.32
  153.2 5.8 collective-permute-start.20
  160.5 1.9 collective-permute-start.23
  162.4 6.0 %collective-permute-start.22 = (f32[4,6,1,128]{3,2,1,0:T(1,128)}, f32[4,6,1,128]{3,2,1,0:T(1,128)}, u32[]{:S(2)}, u32[]{:S(2)}) collective-permute-start(f32[4,6,1,128]{3,2,1,0:T(1,128)} %get-tuple-element.112), channel_id=1, source_target_pairs={{0,1},{1,2},{2,3},{4,5},{5,6},{6,7},{8,9},{9,10},{10,11},{12,13},{... | collective-permute-start | bytes 36872 | tf_op jit(solution)/shard_map/ppermute | solution.py:20
  172.6 4.1 collective-permute-start.24
  177.6 1.9 collective-permute-start.27
  179.5 6.0 %collective-permute-start.26 = (f32[4,6,1,128]{3,2,1,0:T(1,128)S(1)}, f32[4,6,1,128]{3,2,1,0:T(1,128)S(1)}, u32[]{:S(2)}, u32[]{:S(2)}) collective-permute-start(f32[4,6,1,128]{3,2,1,0:T(1,128)S(1)} %get-tuple-element.110), channel_id=1, source_target_pairs={{0,1},{1,2},{2,3},{4,5},{5,6},{6,7},{8,9},{9,10},{10,11},{12,13},{... | collective-permute-start | bytes 36872 | tf_op jit(solution)/shard_map/ppermute | solution.py:20
  185.6 1.3 collective-permute-done.26
  188.6 5.2 collective-permute-start.28
  194.7 1.9 collective-permute-start.31
  196.6 6.0 %collective-permute-start.30 = (f32[4,6,1,128]{3,2,1,0:T(1,128)S(1)}, f32[4,6,1,128]{3,2,1,0:T(1,128)S(1)}, u32[]{:S(2)}, u32[]{:S(2)}) collective-permute-start(f32[4,6,1,128]{3,2,1,0:T(1,128)S(1)} %get-tuple-element.108), channel_id=1, source_target_pairs={{0,1},{1,2},{2,3},{4,5},{5,6},{6,7},{8,9},{9,10},{10,11},{12,13},{... | collective-permute-start | bytes 36872 | tf_op jit(solution)/shard_map/ppermute | solution.py:20
  202.7 1.9 collective-permute-start.35
  204.6 6.0 %collective-permute-start.34 = (f32[4,6,1,128]{3,2,1,0:T(1,128)S(1)}, f32[4,6,1,128]{3,2,1,0:T(1,128)S(1)}, u32[]{:S(2)}, u32[]{:S(2)}) collective-permute-start(f32[4,6,1,128]{3,2,1,0:T(1,128)S(1)} %get-tuple-element.106), channel_id=1, source_target_pairs={{0,1},{1,2},{2,3},{4,5},{5,6},{6,7},{8,9},{9,10},{10,11},{12,13},{... | collective-permute-start | bytes 36872 | tf_op jit(solution)/shard_map/ppermute | solution.py:20
  212.4 144.6 %psum.14 = f32[4,128]{1,0:T(4,128)S(1)} all-reduce(f32[4,128]{1,0:T(4,128)S(1)} %fusion.300), channel_id=1, replica_groups=mesh['src'=8,'gx'=16,'gy'=4] {'gx','gy'}, use_global_device_ids=true, to_apply=%region_0.1 | all-reduce | flops 512 | bytes 4096 | tf_op jit(solution)/shard_map/psum | solution.py:140
  359.9 3.0 collective-permute-start.36
  363.9 4.6 collective-permute-start.39
  368.5 3.3 collective-permute-start.38
  371.9 3.1 collective-permute-done.38
  376.6 3.0 collective-permute-start.40
  380.6 1.9 collective-permute-start.43
  382.5 6.0 %collective-permute-start.42 = (f32[4,6,1,128]{3,2,1,0:T(1,128)S(1)}, f32[4,6,1,128]{3,2,1,0:T(1,128)S(1)}, u32[]{:S(2)}, u32[]{:S(2)}) collective-permute-start(f32[4,6,1,128]{3,2,1,0:T(1,128)S(1)} %get-tuple-element.102), channel_id=1, source_target_pairs={{0,1},{1,2},{2,3},{4,5},{5,6},{6,7},{8,9},{9,10},{10,11},{12,13},{... | collective-permute-start | bytes 36872 | tf_op jit(solution)/shard_map/ppermute | solution.py:20
  388.5 1.4 collective-permute-done.42
  391.5 4.1 collective-permute-start.44
  396.6 1.9 collective-permute-start.47
  398.5 6.2 %collective-permute-start.46 = (f32[4,6,1,128]{3,2,1,0:T(1,128)S(1)}, f32[4,6,1,128]{3,2,1,0:T(1,128)S(1)}, u32[]{:S(2)}, u32[]{:S(2)}) collective-permute-start(f32[4,6,1,128]{3,2,1,0:T(1,128)S(1)} %get-tuple-element.100), channel_id=1, source_target_pairs={{0,1},{1,2},{2,3},{4,5},{5,6},{6,7},{8,9},{9,10},{10,11},{12,13},{... | collective-permute-start | bytes 36872 | tf_op jit(solution)/shard_map/ppermute | solution.py:20
  407.5 5.9 collective-permute-start.48
  414.3 1.9 collective-permute-start.51
  416.3 6.0 %collective-permute-start.50 = (f32[4,6,1,128]{3,2,1,0:T(1,128)S(1)}, f32[4,6,1,128]{3,2,1,0:T(1,128)S(1)}, u32[]{:S(2)}, u32[]{:S(2)}) collective-permute-start(f32[4,6,1,128]{3,2,1,0:T(1,128)S(1)} %get-tuple-element.98), channel_id=1, source_target_pairs={{0,1},{1,2},{2,3},{4,5},{5,6},{6,7},{8,9},{9,10},{10,11},{12,13},{... | collective-permute-start | bytes 36872 | tf_op jit(solution)/shard_map/ppermute | solution.py:20
  422.3 1.4 collective-permute-done.50
  425.3 5.6 collective-permute-start.52
  431.8 1.9 collective-permute-start.55
  433.7 6.0 %collective-permute-start.54 = (f32[4,6,1,128]{3,2,1,0:T(1,128)S(1)}, f32[4,6,1,128]{3,2,1,0:T(1,128)S(1)}, u32[]{:S(2)}, u32[]{:S(2)}) collective-permute-start(f32[4,6,1,128]{3,2,1,0:T(1,128)S(1)} %get-tuple-element.96), channel_id=1, source_target_pairs={{0,1},{1,2},{2,3},{4,5},{5,6},{6,7},{8,9},{9,10},{10,11},{12,13},{... | collective-permute-start | bytes 36872 | tf_op jit(solution)/shard_map/ppermute | solution.py:20
  439.8 1.4 collective-permute-done.54
  442.8 5.6 collective-permute-start.56
  449.3 1.9 collective-permute-start.59
  451.2 6.0 %collective-permute-start.58 = (f32[4,6,1,128]{3,2,1,0:T(1,128)S(1)}, f32[4,6,1,128]{3,2,1,0:T(1,128)S(1)}, u32[]{:S(2)}, u32[]{:S(2)}) collective-permute-start(f32[4,6,1,128]{3,2,1,0:T(1,128)S(1)} %get-tuple-element.94), channel_id=1, source_target_pairs={{0,1},{1,2},{2,3},{4,5},{5,6},{6,7},{8,9},{9,10},{10,11},{12,13},{... | collective-permute-start | bytes 36872 | tf_op jit(solution)/shard_map/ppermute | solution.py:20
  457.3 1.4 collective-permute-done.58
  460.4 5.7 collective-permute-start.60
  467.2 2.1 collective-permute-start.63
  469.2 6.0 %collective-permute-start.62 = (f32[8,6,1,128]{3,2,1,0:T(1,128)S(1)}, f32[8,6,1,128]{3,2,1,0:T(1,128)S(1)}, u32[]{:S(2)}, u32[]{:S(2)}) collective-permute-start(f32[8,6,1,128]{3,2,1,0:T(1,128)S(1)} %get-tuple-element.82), channel_id=1, source_target_pairs={{0,1},{1,2},{2,3},{4,5},{5,6},{6,7},{8,9},{9,10},{10,11},{12,13},{... | collective-permute-start | bytes 73736 | tf_op jit(solution)/shard_map/ppermute | solution.py:20
  477.8 106.1 %all-reduce.21.cloned.1.call-done = f32[4,32,128]{2,1,0:T(8,128)} async-done(((f32[4,32,128]{2,1,0:T(8,128)}), f32[4,32,128]{2,1,0:T(8,128)}) %all-reduce.21.cloned.1.call-update) | async-done | bytes 65552 | tf_op jit(solution)/shard_map/psum | solution.py:99
  (203 shorter events, 54.0 us)
Async XLA Ops:
  6.5 577.4 %all-reduce.21.cloned.1.call-start = ((), (), s32[]{:S(2)}) async-start(), calls=%async_computation | async-start | bytes 131072 | tf_op jit(solution)/shard_map/psum | solution.py:99
  36.5 13.1 %collective-permute-start.1 = (f32[1,1,32,128]{2,1,3,0:T(1,128)S(1)}, f32[1,1,32,128]{2,1,3,0:T(1,128)S(1)}, u32[]{:S(2)}, u32[]{:S(2)}) collective-permute-start(f32[1,1,32,128]{2,1,3,0:T(1,128)S(1)} %get-tuple-element.153), channel_id=1, source_target_pairs={{4,0},{8,4},{12,8},{16,12},{20,16},{24,20},{28,24},{32,28},{36,32}... | collective-permute-start | bytes 49160 | tf_op jit(solution)/shard_map/ppermute | solution.py:23
  37.8 11.8 %collective-permute-start = (f32[1,1,32,128]{2,1,3,0:T(1,128)S(1)}, f32[1,1,32,128]{2,1,3,0:T(1,128)S(1)}, u32[]{:S(2)}, u32[]{:S(2)}) collective-permute-start(f32[1,1,32,128]{2,1,3,0:T(1,128)S(1)} %get-tuple-element.152), channel_id=1, source_target_pairs={{0,4},{4,8},{8,12},{12,16},{16,20},{20,24},{24,28},{28,32},{32,36}... | collective-permute-start | bytes 49160 | tf_op jit(solution)/shard_map/ppermute | solution.py:20
  40.9 41.4 %collective-permute-start.4 = (f32[4,1,32,128]{3,2,1,0:T(8,128)S(1)}, f32[4,1,32,128]{3,2,1,0:T(8,128)S(1)}, u32[]{:S(2)}, u32[]{:S(2)}) collective-permute-start(f32[4,1,32,128]{3,2,1,0:T(8,128)S(1)} %get-tuple-element.151), channel_id=1, source_target_pairs={{0,4},{4,8},{8,12},{12,16},{16,20},{20,24},{24,28},{28,32},{32,36}... | collective-permute-start | bytes 196616 | tf_op jit(solution)/shard_map/ppermute | solution.py:20
  44.8 37.5 %collective-permute-start.5 = (f32[4,1,32,128]{3,2,1,0:T(8,128)S(1)}, f32[4,1,32,128]{3,2,1,0:T(8,128)S(1)}, u32[]{:S(2)}, u32[]{:S(2)}) collective-permute-start(f32[4,1,32,128]{3,2,1,0:T(8,128)S(1)} %get-tuple-element.150), channel_id=1, source_target_pairs={{4,0},{8,4},{12,8},{16,12},{20,16},{24,20},{28,24},{32,28},{36,32}... | collective-permute-start | bytes 196616 | tf_op jit(solution)/shard_map/ppermute | solution.py:23
  50.0 29.9 %collective-permute-start.3 = (f32[1,6,1,128]{2,1,3,0:T(8,128)S(1)}, f32[1,6,1,128]{2,1,3,0:T(8,128)S(1)}, u32[]{:S(2)}, u32[]{:S(2)}) collective-permute-start(f32[1,6,1,128]{2,1,3,0:T(8,128)S(1)} %get-tuple-element.93), channel_id=1, source_target_pairs={{1,0},{2,1},{3,2},{5,4},{6,5},{7,6},{9,8},{10,9},{11,10},{13,12},{... | collective-permute-start | bytes 9224 | tf_op jit(solution)/shard_map/ppermute | solution.py:23
  55.4 24.5 %collective-permute-start.2 = (f32[1,6,1,128]{2,1,3,0:T(8,128)S(1)}, f32[1,6,1,128]{2,1,3,0:T(8,128)S(1)}, u32[]{:S(2)}, u32[]{:S(2)}) collective-permute-start(f32[1,6,1,128]{2,1,3,0:T(8,128)S(1)} %get-tuple-element.92), channel_id=1, source_target_pairs={{0,1},{1,2},{2,3},{4,5},{5,6},{6,7},{8,9},{9,10},{10,11},{12,13},{... | collective-permute-start | bytes 9224 | tf_op jit(solution)/shard_map/ppermute | solution.py:20
  82.3 11.8 %collective-permute-start.7 = (f32[4,6,1,128]{3,2,1,0:T(1,128)S(1)}, f32[4,6,1,128]{3,2,1,0:T(1,128)S(1)}, u32[]{:S(2)}, u32[]{:S(2)}) collective-permute-start(f32[4,6,1,128]{3,2,1,0:T(1,128)S(1)} %get-tuple-element.121), channel_id=1, source_target_pairs={{1,0},{2,1},{3,2},{5,4},{6,5},{7,6},{9,8},{10,9},{11,10},{13,12},{... | collective-permute-start | bytes 36872 | tf_op jit(solution)/shard_map/ppermute | solution.py:23
  84.7 9.4 %collective-permute-start.6 = (f32[4,6,1,128]{3,2,1,0:T(1,128)S(1)}, f32[4,6,1,128]{3,2,1,0:T(1,128)S(1)}, u32[]{:S(2)}, u32[]{:S(2)}) collective-permute-start(f32[4,6,1,128]{3,2,1,0:T(1,128)S(1)} %get-tuple-element.120), channel_id=1, source_target_pairs={{0,1},{1,2},{2,3},{4,5},{5,6},{6,7},{8,9},{9,10},{10,11},{12,13},{... | collective-permute-start | bytes 36872 | tf_op jit(solution)/shard_map/ppermute | solution.py:20
  95.2 4.3 collective-permute-start.9
  96.5 3.9 collective-permute-start.8
  100.5 8.0 %collective-permute-start.11 = (f32[4,6,1,128]{3,2,1,0:T(1,128)S(1)}, f32[4,6,1,128]{3,2,1,0:T(1,128)S(1)}, u32[]{:S(2)}, u32[]{:S(2)}) collective-permute-start(f32[4,6,1,128]{3,2,1,0:T(1,128)S(1)} %get-tuple-element.119), channel_id=1, source_target_pairs={{1,0},{2,1},{3,2},{5,4},{6,5},{7,6},{9,8},{10,9},{11,10},{13,12},{... | collective-permute-start | bytes 36872 | tf_op jit(solution)/shard_map/ppermute | solution.py:23
  102.4 7.4 %collective-permute-start.10 = (f32[4,6,1,128]{3,2,1,0:T(1,128)S(1)}, f32[4,6,1,128]{3,2,1,0:T(1,128)S(1)}, u32[]{:S(2)}, u32[]{:S(2)}) collective-permute-start(f32[4,6,1,128]{3,2,1,0:T(1,128)S(1)} %get-tuple-element.118), channel_id=1, source_target_pairs={{0,1},{1,2},{2,3},{4,5},{5,6},{6,7},{8,9},{9,10},{10,11},{12,13},{... | collective-permute-start | bytes 36872 | tf_op jit(solution)/shard_map/ppermute | solution.py:20
  110.1 7.1 %collective-permute-start.13 = (f32[4,1,32,128]{3,2,1,0:T(8,128)S(1)}, f32[4,1,32,128]{3,2,1,0:T(8,128)S(1)}, u32[]{:S(2)}, u32[]{:S(2)}) collective-permute-start(f32[4,1,32,128]{3,2,1,0:T(8,128)S(1)} %get-tuple-element.147), channel_id=1, source_target_pairs={{4,0},{8,4},{12,8},{16,12},{20,16},{24,20},{28,24},{32,28},{36,32}... | collective-permute-start | bytes 196616 | tf_op jit(solution)/shard_map/ppermute | solution.py:23
  111.4 6.7 %collective-permute-start.12 = (f32[4,1,32,128]{3,2,1,0:T(8,128)S(1)}, f32[4,1,32,128]{3,2,1,0:T(8,128)S(1)}, u32[]{:S(2)}, u32[]{:S(2)}) collective-permute-start(f32[4,1,32,128]{3,2,1,0:T(8,128)S(1)} %get-tuple-element.146), channel_id=1, source_target_pairs={{0,4},{4,8},{8,12},{12,16},{16,20},{20,24},{24,28},{28,32},{32,36}... | collective-permute-start | bytes 196616 | tf_op jit(solution)/shard_map/ppermute | solution.py:20
  118.2 8.0 %collective-permute-start.15 = (f32[4,6,1,128]{3,2,1,0:T(1,128)S(1)}, f32[4,6,1,128]{3,2,1,0:T(1,128)S(1)}, u32[]{:S(2)}, u32[]{:S(2)}) collective-permute-start(f32[4,6,1,128]{3,2,1,0:T(1,128)S(1)} %get-tuple-element.117), channel_id=1, source_target_pairs={{1,0},{2,1},{3,2},{5,4},{6,5},{7,6},{9,8},{10,9},{11,10},{13,12},{... | collective-permute-start | bytes 36872 | tf_op jit(solution)/shard_map/ppermute | solution.py:23
  120.1 7.4 %collective-permute-start.14 = (f32[4,6,1,128]{3,2,1,0:T(1,128)S(1)}, f32[4,6,1,128]{3,2,1,0:T(1,128)S(1)}, u32[]{:S(2)}, u32[]{:S(2)}) collective-permute-start(f32[4,6,1,128]{3,2,1,0:T(1,128)S(1)} %get-tuple-element.116), channel_id=1, source_target_pairs={{0,1},{1,2},{2,3},{4,5},{5,6},{6,7},{8,9},{9,10},{10,11},{12,13},{... | collective-permute-start | bytes 36872 | tf_op jit(solution)/shard_map/ppermute | solution.py:20
  127.8 7.3 %collective-permute-start.17 = (f32[4,1,32,128]{3,2,1,0:T(8,128)S(1)}, f32[4,1,32,128]{3,2,1,0:T(8,128)S(1)}, u32[]{:S(2)}, u32[]{:S(2)}) collective-permute-start(f32[4,1,32,128]{3,2,1,0:T(8,128)S(1)} %get-tuple-element.145), channel_id=1, source_target_pairs={{4,0},{8,4},{12,8},{16,12},{20,16},{24,20},{28,24},{32,28},{36,32}... | collective-permute-start | bytes 196616 | tf_op jit(solution)/shard_map/ppermute | solution.py:23
  129.3 6.8 %collective-permute-start.16 = (f32[4,1,32,128]{3,2,1,0:T(8,128)S(1)}, f32[4,1,32,128]{3,2,1,0:T(8,128)S(1)}, u32[]{:S(2)}, u32[]{:S(2)}) collective-permute-start(f32[4,1,32,128]{3,2,1,0:T(8,128)S(1)} %get-tuple-element.144), channel_id=1, source_target_pairs={{0,4},{4,8},{8,12},{12,16},{16,20},{20,24},{24,28},{28,32},{32,36}... | collective-permute-start | bytes 196616 | tf_op jit(solution)/shard_map/ppermute | solution.py:20
  136.1 15.5 %collective-permute-start.19 = (f32[4,6,1,128]{3,2,1,0:T(1,128)S(1)}, f32[4,6,1,128]{3,2,1,0:T(1,128)S(1)}, u32[]{:S(2)}, u32[]{:S(2)}) collective-permute-start(f32[4,6,1,128]{3,2,1,0:T(1,128)S(1)} %get-tuple-element.115), channel_id=1, source_target_pairs={{1,0},{2,1},{3,2},{5,4},{6,5},{7,6},{9,8},{10,9},{11,10},{13,12},{... | collective-permute-start | bytes 36872 | tf_op jit(solution)/shard_map/ppermute | solution.py:23
  138.0 13.6 %collective-permute-start.18 = (f32[4,6,1,128]{3,2,1,0:T(1,128)S(1)}, f32[4,6,1,128]{3,2,1,0:T(1,128)S(1)}, u32[]{:S(2)}, u32[]{:S(2)}) collective-permute-start(f32[4,6,1,128]{3,2,1,0:T(1,128)S(1)} %get-tuple-element.114), channel_id=1, source_target_pairs={{0,1},{1,2},{2,3},{4,5},{5,6},{6,7},{8,9},{9,10},{10,11},{12,13},{... | collective-permute-start | bytes 36872 | tf_op jit(solution)/shard_map/ppermute | solution.py:20
  144.7 32.0 %collective-permute-start.32 = (f32[4,1,32,128]{3,2,1,0:T(8,128)}, f32[4,1,32,128]{3,2,1,0:T(8,128)S(1)}, u32[]{:S(2)}, u32[]{:S(2)}) collective-permute-start(f32[4,1,32,128]{3,2,1,0:T(8,128)} %get-tuple-element.137), channel_id=1, source_target_pairs={{0,4},{4,8},{8,12},{12,16},{16,20},{20,24},{24,28},{28,32},{32,36}... | collective-permute-start | bytes 196616 | tf_op jit(solution)/shard_map/ppermute | solution.py:20
  150.2 43.6 %collective-permute-start.33 = (f32[4,1,32,128]{3,2,1,0:T(8,128)}, f32[4,1,32,128]{3,2,1,0:T(8,128)}, u32[]{:S(2)}, u32[]{:S(2)}) collective-permute-start(f32[4,1,32,128]{3,2,1,0:T(8,128)} %get-tuple-element.136), channel_id=1, source_target_pairs={{4,0},{8,4},{12,8},{16,12},{20,16},{24,20},{28,24},{32,28},{36,32}... | collective-permute-start | bytes 196616 | tf_op jit(solution)/shard_map/ppermute | solution.py:23
  151.9 7.7 %collective-permute-start.21 = (f32[4,1,32,128]{3,2,1,0:T(8,128)S(1)}, f32[4,1,32,128]{3,2,1,0:T(8,128)S(1)}, u32[]{:S(2)}, u32[]{:S(2)}) collective-permute-start(f32[4,1,32,128]{3,2,1,0:T(8,128)S(1)} %get-tuple-element.143), channel_id=1, source_target_pairs={{4,0},{8,4},{12,8},{16,12},{20,16},{24,20},{28,24},{32,28},{36,32}... | collective-permute-start | bytes 196616 | tf_op jit(solution)/shard_map/ppermute | solution.py:23
  153.2 6.7 %collective-permute-start.20 = (f32[4,1,32,128]{3,2,1,0:T(8,128)S(1)}, f32[4,1,32,128]{3,2,1,0:T(8,128)S(1)}, u32[]{:S(2)}, u32[]{:S(2)}) collective-permute-start(f32[4,1,32,128]{3,2,1,0:T(8,128)S(1)} %get-tuple-element.142), channel_id=1, source_target_pairs={{0,4},{4,8},{8,12},{12,16},{16,20},{20,24},{24,28},{28,32},{32,36}... | collective-permute-start | bytes 196616 | tf_op jit(solution)/shard_map/ppermute | solution.py:20
  160.5 9.8 %collective-permute-start.23 = (f32[4,6,1,128]{3,2,1,0:T(1,128)}, f32[4,6,1,128]{3,2,1,0:T(1,128)}, u32[]{:S(2)}, u32[]{:S(2)}) collective-permute-start(f32[4,6,1,128]{3,2,1,0:T(1,128)} %get-tuple-element.113), channel_id=1, source_target_pairs={{1,0},{2,1},{3,2},{5,4},{6,5},{7,6},{9,8},{10,9},{11,10},{13,12},{... | collective-permute-start | bytes 36872 | tf_op jit(solution)/shard_map/ppermute | solution.py:23
  162.4 7.8 %collective-permute-start.22 = (f32[4,6,1,128]{3,2,1,0:T(1,128)}, f32[4,6,1,128]{3,2,1,0:T(1,128)}, u32[]{:S(2)}, u32[]{:S(2)}) collective-permute-start(f32[4,6,1,128]{3,2,1,0:T(1,128)} %get-tuple-element.112), channel_id=1, source_target_pairs={{0,1},{1,2},{2,3},{4,5},{5,6},{6,7},{8,9},{9,10},{10,11},{12,13},{... | collective-permute-start | bytes 36872 | tf_op jit(solution)/shard_map/ppermute | solution.py:20
  171.3 5.5 collective-permute-start.25
  172.6 5.0 collective-permute-start.24
  177.6 8.0 %collective-permute-start.27 = (f32[4,6,1,128]{3,2,1,0:T(1,128)S(1)}, f32[4,6,1,128]{3,2,1,0:T(1,128)S(1)}, u32[]{:S(2)}, u32[]{:S(2)}) collective-permute-start(f32[4,6,1,128]{3,2,1,0:T(1,128)S(1)} %get-tuple-element.111), channel_id=1, source_target_pairs={{1,0},{2,1},{3,2},{5,4},{6,5},{7,6},{9,8},{10,9},{11,10},{13,12},{... | collective-permute-start | bytes 36872 | tf_op jit(solution)/shard_map/ppermute | solution.py:23
  179.5 7.4 %collective-permute-start.26 = (f32[4,6,1,128]{3,2,1,0:T(1,128)S(1)}, f32[4,6,1,128]{3,2,1,0:T(1,128)S(1)}, u32[]{:S(2)}, u32[]{:S(2)}) collective-permute-start(f32[4,6,1,128]{3,2,1,0:T(1,128)S(1)} %get-tuple-element.110), channel_id=1, source_target_pairs={{0,1},{1,2},{2,3},{4,5},{5,6},{6,7},{8,9},{9,10},{10,11},{12,13},{... | collective-permute-start | bytes 36872 | tf_op jit(solution)/shard_map/ppermute | solution.py:20
  187.3 7.4 %collective-permute-start.29 = (f32[4,1,32,128]{3,2,1,0:T(8,128)S(1)}, f32[4,1,32,128]{3,2,1,0:T(8,128)S(1)}, u32[]{:S(2)}, u32[]{:S(2)}) collective-permute-start(f32[4,1,32,128]{3,2,1,0:T(8,128)S(1)} %get-tuple-element.139), channel_id=1, source_target_pairs={{4,0},{8,4},{12,8},{16,12},{20,16},{24,20},{28,24},{32,28},{36,32}... | collective-permute-start | bytes 196616 | tf_op jit(solution)/shard_map/ppermute | solution.py:23
  188.6 6.1 %collective-permute-start.28 = (f32[4,1,32,128]{3,2,1,0:T(8,128)S(1)}, f32[4,1,32,128]{3,2,1,0:T(8,128)S(1)}, u32[]{:S(2)}, u32[]{:S(2)}) collective-permute-start(f32[4,1,32,128]{3,2,1,0:T(8,128)S(1)} %get-tuple-element.138), channel_id=1, source_target_pairs={{0,4},{4,8},{8,12},{12,16},{16,20},{20,24},{24,28},{28,32},{32,36}... | collective-permute-start | bytes 196616 | tf_op jit(solution)/shard_map/ppermute | solution.py:20
  194.7 16.0 %collective-permute-start.31 = (f32[4,6,1,128]{3,2,1,0:T(1,128)S(1)}, f32[4,6,1,128]{3,2,1,0:T(1,128)S(1)}, u32[]{:S(2)}, u32[]{:S(2)}) collective-permute-start(f32[4,6,1,128]{3,2,1,0:T(1,128)S(1)} %get-tuple-element.109), channel_id=1, source_target_pairs={{1,0},{2,1},{3,2},{5,4},{6,5},{7,6},{9,8},{10,9},{11,10},{13,12},{... | collective-permute-start | bytes 36872 | tf_op jit(solution)/shard_map/ppermute | solution.py:23
  196.6 14.0 %collective-permute-start.30 = (f32[4,6,1,128]{3,2,1,0:T(1,128)S(1)}, f32[4,6,1,128]{3,2,1,0:T(1,128)S(1)}, u32[]{:S(2)}, u32[]{:S(2)}) collective-permute-start(f32[4,6,1,128]{3,2,1,0:T(1,128)S(1)} %get-tuple-element.108), channel_id=1, source_target_pairs={{0,1},{1,2},{2,3},{4,5},{5,6},{6,7},{8,9},{9,10},{10,11},{12,13},{... | collective-permute-start | bytes 36872 | tf_op jit(solution)/shard_map/ppermute | solution.py:20
  202.7 154.8 %collective-permute-start.35 = (f32[4,6,1,128]{3,2,1,0:T(1,128)S(1)}, f32[4,6,1,128]{3,2,1,0:T(1,128)S(1)}, u32[]{:S(2)}, u32[]{:S(2)}) collective-permute-start(f32[4,6,1,128]{3,2,1,0:T(1,128)S(1)} %get-tuple-element.107), channel_id=1, source_target_pairs={{1,0},{2,1},{3,2},{5,4},{6,5},{7,6},{9,8},{10,9},{11,10},{13,12},{... | collective-permute-start | bytes 36872 | tf_op jit(solution)/shard_map/ppermute | solution.py:23
  204.6 152.9 %collective-permute-start.34 = (f32[4,6,1,128]{3,2,1,0:T(1,128)S(1)}, f32[4,6,1,128]{3,2,1,0:T(1,128)S(1)}, u32[]{:S(2)}, u32[]{:S(2)}) collective-permute-start(f32[4,6,1,128]{3,2,1,0:T(1,128)S(1)} %get-tuple-element.106), channel_id=1, source_target_pairs={{0,1},{1,2},{2,3},{4,5},{5,6},{6,7},{8,9},{9,10},{10,11},{12,13},{... | collective-permute-start | bytes 36872 | tf_op jit(solution)/shard_map/ppermute | solution.py:20
  358.6 4.3 collective-permute-start.37
  359.9 3.9 collective-permute-start.36
  363.9 8.0 %collective-permute-start.39 = (f32[4,6,1,128]{3,2,1,0:T(1,128)S(1)}, f32[4,6,1,128]{3,2,1,0:T(1,128)S(1)}, u32[]{:S(2)}, u32[]{:S(2)}) collective-permute-start(f32[4,6,1,128]{3,2,1,0:T(1,128)S(1)} %get-tuple-element.105), channel_id=1, source_target_pairs={{1,0},{2,1},{3,2},{5,4},{6,5},{7,6},{9,8},{10,9},{11,10},{13,12},{... | collective-permute-start | bytes 36872 | tf_op jit(solution)/shard_map/ppermute | solution.py:23
  368.5 6.5 %collective-permute-start.38 = (f32[4,6,1,128]{3,2,1,0:T(1,128)S(1)}, f32[4,6,1,128]{3,2,1,0:T(1,128)S(1)}, u32[]{:S(2)}, u32[]{:S(2)}) collective-permute-start(f32[4,6,1,128]{3,2,1,0:T(1,128)S(1)} %get-tuple-element.104), channel_id=1, source_target_pairs={{0,1},{1,2},{2,3},{4,5},{5,6},{6,7},{8,9},{9,10},{10,11},{12,13},{... | collective-permute-start | bytes 36872 | tf_op jit(solution)/shard_map/ppermute | solution.py:20
  375.3 4.3 collective-permute-start.41
  380.6 8.0 %collective-permute-start.43 = (f32[4,6,1,128]{3,2,1,0:T(1,128)S(1)}, f32[4,6,1,128]{3,2,1,0:T(1,128)S(1)}, u32[]{:S(2)}, u32[]{:S(2)}) collective-permute-start(f32[4,6,1,128]{3,2,1,0:T(1,128)S(1)} %get-tuple-element.103), channel_id=1, source_target_pairs={{1,0},{2,1},{3,2},{5,4},{6,5},{7,6},{9,8},{10,9},{11,10},{13,12},{... | collective-permute-start | bytes 36872 | tf_op jit(solution)/shard_map/ppermute | solution.py:23
  382.5 7.4 %collective-permute-start.42 = (f32[4,6,1,128]{3,2,1,0:T(1,128)S(1)}, f32[4,6,1,128]{3,2,1,0:T(1,128)S(1)}, u32[]{:S(2)}, u32[]{:S(2)}) collective-permute-start(f32[4,6,1,128]{3,2,1,0:T(1,128)S(1)} %get-tuple-element.102), channel_id=1, source_target_pairs={{0,1},{1,2},{2,3},{4,5},{5,6},{6,7},{8,9},{9,10},{10,11},{12,13},{... | collective-permute-start | bytes 36872 | tf_op jit(solution)/shard_map/ppermute | solution.py:20
  390.2 5.4 collective-permute-start.45
  391.5 5.0 collective-permute-start.44
  396.6 8.2 %collective-permute-start.47 = (f32[4,6,1,128]{3,2,1,0:T(1,128)S(1)}, f32[4,6,1,128]{3,2,1,0:T(1,128)S(1)}, u32[]{:S(2)}, u32[]{:S(2)}) collective-permute-start(f32[4,6,1,128]{3,2,1,0:T(1,128)S(1)} %get-tuple-element.101), channel_id=1, source_target_pairs={{1,0},{2,1},{3,2},{5,4},{6,5},{7,6},{9,8},{10,9},{11,10},{13,12},{... | collective-permute-start | bytes 36872 | tf_op jit(solution)/shard_map/ppermute | solution.py:23
  398.5 7.4 %collective-permute-start.46 = (f32[4,6,1,128]{3,2,1,0:T(1,128)S(1)}, f32[4,6,1,128]{3,2,1,0:T(1,128)S(1)}, u32[]{:S(2)}, u32[]{:S(2)}) collective-permute-start(f32[4,6,1,128]{3,2,1,0:T(1,128)S(1)} %get-tuple-element.100), channel_id=1, source_target_pairs={{0,1},{1,2},{2,3},{4,5},{5,6},{6,7},{8,9},{9,10},{10,11},{12,13},{... | collective-permute-start | bytes 36872 | tf_op jit(solution)/shard_map/ppermute | solution.py:20
  406.2 7.2 %collective-permute-start.49 = (f32[4,1,32,128]{3,2,1,0:T(8,128)S(1)}, f32[4,1,32,128]{3,2,1,0:T(8,128)S(1)}, u32[]{:S(2)}, u32[]{:S(2)}) collective-permute-start(f32[4,1,32,128]{3,2,1,0:T(8,128)S(1)} %get-tuple-element.129), channel_id=1, source_target_pairs={{4,0},{8,4},{12,8},{16,12},{20,16},{24,20},{28,24},{32,28},{36,32}... | collective-permute-start | bytes 196616 | tf_op jit(solution)/shard_map/ppermute | solution.py:23
  407.5 6.8 %collective-permute-start.48 = (f32[4,1,32,128]{3,2,1,0:T(8,128)S(1)}, f32[4,1,32,128]{3,2,1,0:T(8,128)S(1)}, u32[]{:S(2)}, u32[]{:S(2)}) collective-permute-start(f32[4,1,32,128]{3,2,1,0:T(8,128)S(1)} %get-tuple-element.128), channel_id=1, source_target_pairs={{0,4},{4,8},{8,12},{12,16},{16,20},{20,24},{24,28},{28,32},{32,36}... | collective-permute-start | bytes 196616 | tf_op jit(solution)/shard_map/ppermute | solution.py:20
  414.3 8.0 %collective-permute-start.51 = (f32[4,6,1,128]{3,2,1,0:T(1,128)S(1)}, f32[4,6,1,128]{3,2,1,0:T(1,128)S(1)}, u32[]{:S(2)}, u32[]{:S(2)}) collective-permute-start(f32[4,6,1,128]{3,2,1,0:T(1,128)S(1)} %get-tuple-element.99), channel_id=1, source_target_pairs={{1,0},{2,1},{3,2},{5,4},{6,5},{7,6},{9,8},{10,9},{11,10},{13,12},{... | collective-permute-start | bytes 36872 | tf_op jit(solution)/shard_map/ppermute | solution.py:23
  416.3 7.4 %collective-permute-start.50 = (f32[4,6,1,128]{3,2,1,0:T(1,128)S(1)}, f32[4,6,1,128]{3,2,1,0:T(1,128)S(1)}, u32[]{:S(2)}, u32[]{:S(2)}) collective-permute-start(f32[4,6,1,128]{3,2,1,0:T(1,128)S(1)} %get-tuple-element.98), channel_id=1, source_target_pairs={{0,1},{1,2},{2,3},{4,5},{5,6},{6,7},{8,9},{9,10},{10,11},{12,13},{... | collective-permute-start | bytes 36872 | tf_op jit(solution)/shard_map/ppermute | solution.py:20
  424.0 6.9 %collective-permute-start.53 = (f32[4,1,32,128]{3,2,1,0:T(8,128)S(1)}, f32[4,1,32,128]{3,2,1,0:T(8,128)S(1)}, u32[]{:S(2)}, u32[]{:S(2)}) collective-permute-start(f32[4,1,32,128]{3,2,1,0:T(8,128)S(1)} %get-tuple-element.127), channel_id=1, source_target_pairs={{4,0},{8,4},{12,8},{16,12},{20,16},{24,20},{28,24},{32,28},{36,32}... | collective-permute-start | bytes 196616 | tf_op jit(solution)/shard_map/ppermute | solution.py:23
  425.3 6.5 %collective-permute-start.52 = (f32[4,1,32,128]{3,2,1,0:T(8,128)S(1)}, f32[4,1,32,128]{3,2,1,0:T(8,128)S(1)}, u32[]{:S(2)}, u32[]{:S(2)}) collective-permute-start(f32[4,1,32,128]{3,2,1,0:T(8,128)S(1)} %get-tuple-element.126), channel_id=1, source_target_pairs={{0,4},{4,8},{8,12},{12,16},{16,20},{20,24},{24,28},{28,32},{32,36}... | collective-permute-start | bytes 196616 | tf_op jit(solution)/shard_map/ppermute | solution.py:20
  431.8 8.0 %collective-permute-start.55 = (f32[4,6,1,128]{3,2,1,0:T(1,128)S(1)}, f32[4,6,1,128]{3,2,1,0:T(1,128)S(1)}, u32[]{:S(2)}, u32[]{:S(2)}) collective-permute-start(f32[4,6,1,128]{3,2,1,0:T(1,128)S(1)} %get-tuple-element.97), channel_id=1, source_target_pairs={{1,0},{2,1},{3,2},{5,4},{6,5},{7,6},{9,8},{10,9},{11,10},{13,12},{... | collective-permute-start | bytes 36872 | tf_op jit(solution)/shard_map/ppermute | solution.py:23
  433.7 7.4 %collective-permute-start.54 = (f32[4,6,1,128]{3,2,1,0:T(1,128)S(1)}, f32[4,6,1,128]{3,2,1,0:T(1,128)S(1)}, u32[]{:S(2)}, u32[]{:S(2)}) collective-permute-start(f32[4,6,1,128]{3,2,1,0:T(1,128)S(1)} %get-tuple-element.96), channel_id=1, source_target_pairs={{0,1},{1,2},{2,3},{4,5},{5,6},{6,7},{8,9},{9,10},{10,11},{12,13},{... | collective-permute-start | bytes 36872 | tf_op jit(solution)/shard_map/ppermute | solution.py:20
  441.5 6.9 %collective-permute-start.57 = (f32[4,1,32,128]{3,2,1,0:T(8,128)S(1)}, f32[4,1,32,128]{3,2,1,0:T(8,128)S(1)}, u32[]{:S(2)}, u32[]{:S(2)}) collective-permute-start(f32[4,1,32,128]{3,2,1,0:T(8,128)S(1)} %get-tuple-element.125), channel_id=1, source_target_pairs={{4,0},{8,4},{12,8},{16,12},{20,16},{24,20},{28,24},{32,28},{36,32}... | collective-permute-start | bytes 196616 | tf_op jit(solution)/shard_map/ppermute | solution.py:23
  442.8 6.5 %collective-permute-start.56 = (f32[4,1,32,128]{3,2,1,0:T(8,128)S(1)}, f32[4,1,32,128]{3,2,1,0:T(8,128)S(1)}, u32[]{:S(2)}, u32[]{:S(2)}) collective-permute-start(f32[4,1,32,128]{3,2,1,0:T(8,128)S(1)} %get-tuple-element.124), channel_id=1, source_target_pairs={{0,4},{4,8},{8,12},{12,16},{16,20},{20,24},{24,28},{28,32},{32,36}... | collective-permute-start | bytes 196616 | tf_op jit(solution)/shard_map/ppermute | solution.py:20
  449.3 8.0 %collective-permute-start.59 = (f32[4,6,1,128]{3,2,1,0:T(1,128)S(1)}, f32[4,6,1,128]{3,2,1,0:T(1,128)S(1)}, u32[]{:S(2)}, u32[]{:S(2)}) collective-permute-start(f32[4,6,1,128]{3,2,1,0:T(1,128)S(1)} %get-tuple-element.95), channel_id=1, source_target_pairs={{1,0},{2,1},{3,2},{5,4},{6,5},{7,6},{9,8},{10,9},{11,10},{13,12},{... | collective-permute-start | bytes 36872 | tf_op jit(solution)/shard_map/ppermute | solution.py:23
  451.2 7.4 %collective-permute-start.58 = (f32[4,6,1,128]{3,2,1,0:T(1,128)S(1)}, f32[4,6,1,128]{3,2,1,0:T(1,128)S(1)}, u32[]{:S(2)}, u32[]{:S(2)}) collective-permute-start(f32[4,6,1,128]{3,2,1,0:T(1,128)S(1)} %get-tuple-element.94), channel_id=1, source_target_pairs={{0,1},{1,2},{2,3},{4,5},{5,6},{6,7},{8,9},{9,10},{10,11},{12,13},{... | collective-permute-start | bytes 36872 | tf_op jit(solution)/shard_map/ppermute | solution.py:20
  459.1 7.1 %collective-permute-start.61 = (f32[8,1,32,128]{3,2,1,0:T(8,128)S(1)}, f32[8,1,32,128]{3,2,1,0:T(8,128)S(1)}, u32[]{:S(2)}, u32[]{:S(2)}) collective-permute-start(f32[8,1,32,128]{3,2,1,0:T(8,128)S(1)} %get-tuple-element.91), channel_id=1, source_target_pairs={{4,0},{8,4},{12,8},{16,12},{20,16},{24,20},{28,24},{32,28},{36,32}... | collective-permute-start | bytes 393224 | tf_op jit(solution)/shard_map/ppermute | solution.py:23
  460.4 6.7 %collective-permute-start.60 = (f32[8,1,32,128]{3,2,1,0:T(8,128)S(1)}, f32[8,1,32,128]{3,2,1,0:T(8,128)S(1)}, u32[]{:S(2)}, u32[]{:S(2)}) collective-permute-start(f32[8,1,32,128]{3,2,1,0:T(8,128)S(1)} %get-tuple-element.90), channel_id=1, source_target_pairs={{0,4},{4,8},{8,12},{12,16},{16,20},{20,24},{24,28},{28,32},{32,36}... | collective-permute-start | bytes 393224 | tf_op jit(solution)/shard_map/ppermute | solution.py:20
  467.2 8.8 %collective-permute-start.63 = (f32[8,6,1,128]{3,2,1,0:T(1,128)S(1)}, f32[8,6,1,128]{3,2,1,0:T(1,128)S(1)}, u32[]{:S(2)}, u32[]{:S(2)}) collective-permute-start(f32[8,6,1,128]{3,2,1,0:T(1,128)S(1)} %get-tuple-element.83), channel_id=1, source_target_pairs={{1,0},{2,1},{3,2},{5,4},{6,5},{7,6},{9,8},{10,9},{11,10},{13,12},{... | collective-permute-start | bytes 73736 | tf_op jit(solution)/shard_map/ppermute | solution.py:23
  469.2 7.5 %collective-permute-start.62 = (f32[8,6,1,128]{3,2,1,0:T(1,128)S(1)}, f32[8,6,1,128]{3,2,1,0:T(1,128)S(1)}, u32[]{:S(2)}, u32[]{:S(2)}) collective-permute-start(f32[8,6,1,128]{3,2,1,0:T(1,128)S(1)} %get-tuple-element.82), channel_id=1, source_target_pairs={{0,1},{1,2},{2,3},{4,5},{5,6},{6,7},{8,9},{9,10},{10,11},{12,13},{... | collective-permute-start | bytes 73736 | tf_op jit(solution)/shard_map/ppermute | solution.py:20
  (22 other events, 714.6 us)
Sparse Core Ops, SparseCore 0:
  477.9 105.9 all-reduce.20
where the time goes:
time: 595 us; the launch traced here: 592 us
  starting transfers between devices  224 us (38%)
  blocking collectives  174 us (29%)
  waiting for transfers between devices  153 us (26%)
  other arithmetic  15 us (3%)
  between operations  14.6 us (2%)
  local copies, waits for them, and re-layouts  12.1 us (2%)
    ppermute x32, starting transfers between devices, padded_2(): lax.ppermute(lax.slice_in_dim(block, block.shape[dim] - width, None, axis...  166 us
    psum x1, blocking collectives, body(): predicted = lax.psum(local_values, ('gx', 'gy'))  145 us
    psum x1, waiting for transfers between devices, reduce_groups(): summed = lax.psum(partial_value, 'src')  106 us
    ppermute x32, starting transfers between devices, padded_2(): lax.ppermute(lax.slice_in_dim(block, 0, width, axis=dim), axis, backward)  58.2 us
    all_gather x1, blocking collectives, body(): panel = lax.all_gather(conductivity, 'src', axis=2, tiled=True)  29 us
    ppermute x32, waiting for transfers between devices, padded_2(): lax.ppermute(lax.slice_in_dim(block, block.shape[dim] - width, None, axis...  24.7 us
    ppermute x32, waiting for transfers between devices, padded_2(): lax.ppermute(lax.slice_in_dim(block, 0, width, axis=dim), axis, backward)  22 us
  transfers between devices with their start and end apart: 65, of which 24 were waited for; matrix products, arithmetic and copies ran while one was open for 3% of the time, Pallas kernels for 0%

commit v1 on v0

--- a/solution.py
+++ b/solution.py
@@ -137,7 +137,8 @@
     local_values = jnp.dot(
         top, pickup.T, precision=lax.Precision.HIGHEST, preferred_element_type=jnp.float32
     )
-    predicted = lax.psum(local_values, ("gx", "gy"))
+    half = lax.psum(local_values, "gx")
+    predicted = lax.psum(half, "gy")
     misfit = predicted - rows_observed
     back = jnp.dot(
         misfit, pickup, precision=lax.Precision.HIGHEST, preferred_element_type=jnp.float32

time: 595 us -> 488 us (0.82)
  blocking collectives: 174 us -> 72.3 us
  waiting for transfers between devices: 153 us -> 147 us
    psum x1 -> x2, blocking collectives: 145 us -> 43.3 us  [the longest x1 34.2 us: body(): half = lax.psum(local_values, 'gx')]
where the time goes in v1:
time: 488 us; the launch traced here: 486 us
  starting transfers between devices  224 us (46%)
  waiting for transfers between devices  147 us (30%)
  blocking collectives  72.3 us (15%)
  other arithmetic  15 us (3%)
  between operations  14.6 us (3%)
  local copies, waits for them, and re-layouts  12.1 us (2%)
    ppermute x32, starting transfers between devices, padded_2(): lax.ppermute(lax.slice_in_dim(block, block.shape[dim] - width, None, axis...  167 us
    psum x1, waiting for transfers between devices, reduce_groups(): summed = lax.psum(partial_value, 'src')  101 us
    ppermute x32, starting transfers between devices, padded_2(): lax.ppermute(lax.slice_in_dim(block, 0, width, axis=dim), axis, backward)  57.9 us
    psum x1, blocking collectives, body(): half = lax.psum(local_values, 'gx')  34.2 us
    all_gather x1, blocking collectives, body(): panel = lax.all_gather(conductivity, 'src', axis=2, tiled=True)  29 us
    ppermute x32, waiting for transfers between devices, padded_2(): lax.ppermute(lax.slice_in_dim(block, block.shape[dim] - width, None, axis...  24.4 us
    ppermute x32, waiting for transfers between devices, padded_2(): lax.ppermute(lax.slice_in_dim(block, 0, width, axis=dim), axis, backward)  22 us
  transfers between devices with their start and end apart: 65, of which 24 were waited for; matrix products, arithmetic and copies ran while one was open for 3% of the time, Pallas kernels for 0%

profile of v1, /device:TPU:16, one launch (start us, length us, event | category | flops | bytes accessed | tf_op | source)
XLA Modules:
  0.0 486.2 jit_solution(16950973486809533254)
XLA Ops:
  7.3 29.0 %all_gather.3 = f32[4,32,128]{1,0,2:T(4,128)S(1)} all-gather(f32[4,32,16]{1,0,2:T(4,128)S(1)} %copy.69), channel_id=1, replica_groups=mesh['src'=8,'gx'=16,'gy'=4] {'src'}, dimensions={2}, use_global_device_ids=true | all-gather | bytes 73728 | tf_op jit(solution)/shard_map/all_gather | solution.py:104
  37.8 3.0 collective-permute-start
  40.9 3.9 collective-permute-start.4
  50.0 5.4 %collective-permute-start.3 = (f32[1,6,1,128]{2,1,3,0:T(8,128)S(1)}, f32[1,6,1,128]{2,1,3,0:T(8,128)S(1)}, u32[]{:S(2)}, u32[]{:S(2)}) collective-permute-start(f32[1,6,1,128]{2,1,3,0:T(8,128)S(1)} %get-tuple-element.93), channel_id=1, source_target_pairs={{1,0},{2,1},{3,2},{5,4},{6,5},{7,6},{9,8},{10,9},{11,10},{13,12},{... | collective-permute-start | bytes 9224 | tf_op jit(solution)/shard_map/ppermute | solution.py:23
  55.4 2.6 collective-permute-start.2
  58.0 21.9 %collective-permute-done.3 = f32[1,6,1,128]{2,1,3,0:T(8,128)S(1)} collective-permute-done((f32[1,6,1,128]{2,1,3,0:T(8,128)S(1)}, f32[1,6,1,128]{2,1,3,0:T(8,128)S(1)}, u32[]{:S(2)}, u32[]{:S(2)}) %collective-permute-start.3) | collective-permute-done | bytes 3104 | tf_op jit(solution)/shard_map/ppermute | solution.py:23
  80.5 1.8 fusion.293
  82.3 2.3 collective-permute-start.7
  84.7 5.6 %collective-permute-start.6 = (f32[4,6,1,128]{3,2,1,0:T(1,128)S(1)}, f32[4,6,1,128]{3,2,1,0:T(1,128)S(1)}, u32[]{:S(2)}, u32[]{:S(2)}) collective-permute-start(f32[4,6,1,128]{3,2,1,0:T(1,128)S(1)} %get-tuple-element.120), channel_id=1, source_target_pairs={{0,1},{1,2},{2,3},{4,5},{5,6},{6,7},{8,9},{9,10},{10,11},{12,13},{... | collective-permute-start | bytes 36872 | tf_op jit(solution)/shard_map/ppermute | solution.py:20
  90.3 2.0 add_divide_fusion
  96.5 3.0 collective-permute-start.8
  100.5 1.9 collective-permute-start.11
  102.4 6.0 %collective-permute-start.10 = (f32[4,6,1,128]{3,2,1,0:T(1,128)S(1)}, f32[4,6,1,128]{3,2,1,0:T(1,128)S(1)}, u32[]{:S(2)}, u32[]{:S(2)}) collective-permute-start(f32[4,6,1,128]{3,2,1,0:T(1,128)S(1)} %get-tuple-element.118), channel_id=1, source_target_pairs={{0,1},{1,2},{2,3},{4,5},{5,6},{6,7},{8,9},{9,10},{10,11},{12,13},{... | collective-permute-start | bytes 36872 | tf_op jit(solution)/shard_map/ppermute | solution.py:20
  108.5 1.4 collective-permute-done.10
  111.4 5.8 %collective-permute-start.12 = (f32[4,1,32,128]{3,2,1,0:T(8,128)S(1)}, f32[4,1,32,128]{3,2,1,0:T(8,128)S(1)}, u32[]{:S(2)}, u32[]{:S(2)}) collective-permute-start(f32[4,1,32,128]{3,2,1,0:T(8,128)S(1)} %get-tuple-element.146), channel_id=1, source_target_pairs={{0,4},{4,8},{8,12},{12,16},{16,20},{20,24},{24,28},{28,32},{32,36}... | collective-permute-start | bytes 196616 | tf_op jit(solution)/shard_map/ppermute | solution.py:20
  118.2 1.9 collective-permute-start.15
  120.1 6.0 %collective-permute-start.14 = (f32[4,6,1,128]{3,2,1,0:T(1,128)S(1)}, f32[4,6,1,128]{3,2,1,0:T(1,128)S(1)}, u32[]{:S(2)}, u32[]{:S(2)}) collective-permute-start(f32[4,6,1,128]{3,2,1,0:T(1,128)S(1)} %get-tuple-element.116), channel_id=1, source_target_pairs={{0,1},{1,2},{2,3},{4,5},{5,6},{6,7},{8,9},{9,10},{10,11},{12,13},{... | collective-permute-start | bytes 36872 | tf_op jit(solution)/shard_map/ppermute | solution.py:20
  126.2 1.4 collective-permute-done.14
  127.8 1.4 collective-permute-start.17
  129.3 5.9 %collective-permute-start.16 = (f32[4,1,32,128]{3,2,1,0:T(8,128)S(1)}, f32[4,1,32,128]{3,2,1,0:T(8,128)S(1)}, u32[]{:S(2)}, u32[]{:S(2)}) collective-permute-start(f32[4,1,32,128]{3,2,1,0:T(8,128)S(1)} %get-tuple-element.144), channel_id=1, source_target_pairs={{0,4},{4,8},{8,12},{12,16},{16,20},{20,24},{24,28},{28,32},{32,36}... | collective-permute-start | bytes 196616 | tf_op jit(solution)/shard_map/ppermute | solution.py:20
  136.1 1.9 collective-permute-start.19
  138.0 6.0 %collective-permute-start.18 = (f32[4,6,1,128]{3,2,1,0:T(1,128)S(1)}, f32[4,6,1,128]{3,2,1,0:T(1,128)S(1)}, u32[]{:S(2)}, u32[]{:S(2)}) collective-permute-start(f32[4,6,1,128]{3,2,1,0:T(1,128)S(1)} %get-tuple-element.114), channel_id=1, source_target_pairs={{0,1},{1,2},{2,3},{4,5},{5,6},{6,7},{8,9},{9,10},{10,11},{12,13},{... | collective-permute-start | bytes 36872 | tf_op jit(solution)/shard_map/ppermute | solution.py:20
  144.7 5.5 %collective-permute-start.32 = (f32[4,1,32,128]{3,2,1,0:T(8,128)}, f32[4,1,32,128]{3,2,1,0:T(8,128)S(1)}, u32[]{:S(2)}, u32[]{:S(2)}) collective-permute-start(f32[4,1,32,128]{3,2,1,0:T(8,128)} %get-tuple-element.137), channel_id=1, source_target_pairs={{0,4},{4,8},{8,12},{12,16},{16,20},{20,24},{24,28},{28,32},{32,36}... | collective-permute-start | bytes 196616 | tf_op jit(solution)/shard_map/ppermute | solution.py:20
  153.2 5.8 %collective-permute-start.20 = (f32[4,1,32,128]{3,2,1,0:T(8,128)S(1)}, f32[4,1,32,128]{3,2,1,0:T(8,128)S(1)}, u32[]{:S(2)}, u32[]{:S(2)}) collective-permute-start(f32[4,1,32,128]{3,2,1,0:T(8,128)S(1)} %get-tuple-element.142), channel_id=1, source_target_pairs={{0,4},{4,8},{8,12},{12,16},{16,20},{20,24},{24,28},{28,32},{32,36}... | collective-permute-start | bytes 196616 | tf_op jit(solution)/shard_map/ppermute | solution.py:20
  160.5 1.9 collective-permute-start.23
  162.4 6.0 %collective-permute-start.22 = (f32[4,6,1,128]{3,2,1,0:T(1,128)}, f32[4,6,1,128]{3,2,1,0:T(1,128)}, u32[]{:S(2)}, u32[]{:S(2)}) collective-permute-start(f32[4,6,1,128]{3,2,1,0:T(1,128)} %get-tuple-element.112), channel_id=1, source_target_pairs={{0,1},{1,2},{2,3},{4,5},{5,6},{6,7},{8,9},{9,10},{10,11},{12,13},{... | collective-permute-start | bytes 36872 | tf_op jit(solution)/shard_map/ppermute | solution.py:20
  172.6 4.1 collective-permute-start.24
  177.7 1.9 collective-permute-start.27
  179.6 6.0 %collective-permute-start.26 = (f32[4,6,1,128]{3,2,1,0:T(1,128)S(1)}, f32[4,6,1,128]{3,2,1,0:T(1,128)S(1)}, u32[]{:S(2)}, u32[]{:S(2)}) collective-permute-start(f32[4,6,1,128]{3,2,1,0:T(1,128)S(1)} %get-tuple-element.110), channel_id=1, source_target_pairs={{0,1},{1,2},{2,3},{4,5},{5,6},{6,7},{8,9},{9,10},{10,11},{12,13},{... | collective-permute-start | bytes 36872 | tf_op jit(solution)/shard_map/ppermute | solution.py:20
  188.6 5.2 %collective-permute-start.28 = (f32[4,1,32,128]{3,2,1,0:T(8,128)S(1)}, f32[4,1,32,128]{3,2,1,0:T(8,128)S(1)}, u32[]{:S(2)}, u32[]{:S(2)}) collective-permute-start(f32[4,1,32,128]{3,2,1,0:T(8,128)S(1)} %get-tuple-element.138), channel_id=1, source_target_pairs={{0,4},{4,8},{8,12},{12,16},{16,20},{20,24},{24,28},{28,32},{32,36}... | collective-permute-start | bytes 196616 | tf_op jit(solution)/shard_map/ppermute | solution.py:20
  194.7 1.9 collective-permute-start.31
  196.6 6.0 %collective-permute-start.30 = (f32[4,6,1,128]{3,2,1,0:T(1,128)S(1)}, f32[4,6,1,128]{3,2,1,0:T(1,128)S(1)}, u32[]{:S(2)}, u32[]{:S(2)}) collective-permute-start(f32[4,6,1,128]{3,2,1,0:T(1,128)S(1)} %get-tuple-element.108), channel_id=1, source_target_pairs={{0,1},{1,2},{2,3},{4,5},{5,6},{6,7},{8,9},{9,10},{10,11},{12,13},{... | collective-permute-start | bytes 36872 | tf_op jit(solution)/shard_map/ppermute | solution.py:20
  202.7 1.9 collective-permute-start.35
  204.6 6.0 %collective-permute-start.34 = (f32[4,6,1,128]{3,2,1,0:T(1,128)S(1)}, f32[4,6,1,128]{3,2,1,0:T(1,128)S(1)}, u32[]{:S(2)}, u32[]{:S(2)}) collective-permute-start(f32[4,6,1,128]{3,2,1,0:T(1,128)S(1)} %get-tuple-element.106), channel_id=1, source_target_pairs={{0,1},{1,2},{2,3},{4,5},{5,6},{6,7},{8,9},{9,10},{10,11},{12,13},{... | collective-permute-start | bytes 36872 | tf_op jit(solution)/shard_map/ppermute | solution.py:20
  212.4 34.2 %psum.21 = f32[4,128]{1,0:T(4,128)S(1)} all-reduce(f32[4,128]{1,0:T(4,128)S(1)} %fusion.300), channel_id=1, replica_groups=mesh['src'=8,'gx'=16,'gy'=4] {'gx'}, use_global_device_ids=true, to_apply=%region_0.1 | all-reduce | flops 512 | bytes 4096 | tf_op jit(solution)/shard_map/psum | solution.py:140
  246.5 9.1 %psum.22 = f32[4,128]{1,0:T(4,128)S(1)} all-reduce(f32[4,128]{1,0:T(4,128)S(1)} %psum.21), channel_id=1, replica_groups=mesh['src'=8,'gx'=16,'gy'=4] {'gy'}, use_global_device_ids=true, to_apply=%region_1.2 | all-reduce | flops 512 | bytes 4096 | tf_op jit(solution)/shard_map/psum | solution.py:141
  258.6 3.0 collective-permute-start.36
  262.6 4.3 collective-permute-start.39
  266.9 3.6 collective-permute-start.38
  270.5 2.9 collective-permute-done.38
  275.0 3.0 collective-permute-start.40
  279.0 1.9 collective-permute-start.43
  280.9 6.0 %collective-permute-start.42 = (f32[4,6,1,128]{3,2,1,0:T(1,128)S(1)}, f32[4,6,1,128]{3,2,1,0:T(1,128)S(1)}, u32[]{:S(2)}, u32[]{:S(2)}) collective-permute-start(f32[4,6,1,128]{3,2,1,0:T(1,128)S(1)} %get-tuple-element.102), channel_id=1, source_target_pairs={{0,1},{1,2},{2,3},{4,5},{5,6},{6,7},{8,9},{9,10},{10,11},{12,13},{... | collective-permute-start | bytes 36872 | tf_op jit(solution)/shard_map/ppermute | solution.py:20
  286.9 1.4 collective-permute-done.42
  289.9 5.0 %collective-permute-start.44 = (f32[4,1,32,128]{3,2,1,0:T(8,128)S(1)}, f32[4,1,32,128]{3,2,1,0:T(8,128)S(1)}, u32[]{:S(2)}, u32[]{:S(2)}) collective-permute-start(f32[4,1,32,128]{3,2,1,0:T(8,128)S(1)} %get-tuple-element.130), channel_id=1, source_target_pairs={{0,4},{4,8},{8,12},{12,16},{16,20},{20,24},{24,28},{28,32},{32,36}... | collective-permute-start | bytes 196616 | tf_op jit(solution)/shard_map/ppermute | solution.py:20
  295.7 1.9 collective-permute-start.47
  297.6 6.0 %collective-permute-start.46 = (f32[4,6,1,128]{3,2,1,0:T(1,128)S(1)}, f32[4,6,1,128]{3,2,1,0:T(1,128)S(1)}, u32[]{:S(2)}, u32[]{:S(2)}) collective-permute-start(f32[4,6,1,128]{3,2,1,0:T(1,128)S(1)} %get-tuple-element.100), channel_id=1, source_target_pairs={{0,1},{1,2},{2,3},{4,5},{5,6},{6,7},{8,9},{9,10},{10,11},{12,13},{... | collective-permute-start | bytes 36872 | tf_op jit(solution)/shard_map/ppermute | solution.py:20
  303.6 1.4 collective-permute-done.46
  306.6 6.0 %collective-permute-start.48 = (f32[4,1,32,128]{3,2,1,0:T(8,128)S(1)}, f32[4,1,32,128]{3,2,1,0:T(8,128)S(1)}, u32[]{:S(2)}, u32[]{:S(2)}) collective-permute-start(f32[4,1,32,128]{3,2,1,0:T(8,128)S(1)} %get-tuple-element.128), channel_id=1, source_target_pairs={{0,4},{4,8},{8,12},{12,16},{16,20},{20,24},{24,28},{28,32},{32,36}... | collective-permute-start | bytes 196616 | tf_op jit(solution)/shard_map/ppermute | solution.py:20
  313.5 1.9 collective-permute-start.51
  315.5 6.0 %collective-permute-start.50 = (f32[4,6,1,128]{3,2,1,0:T(1,128)S(1)}, f32[4,6,1,128]{3,2,1,0:T(1,128)S(1)}, u32[]{:S(2)}, u32[]{:S(2)}) collective-permute-start(f32[4,6,1,128]{3,2,1,0:T(1,128)S(1)} %get-tuple-element.98), channel_id=1, source_target_pairs={{0,1},{1,2},{2,3},{4,5},{5,6},{6,7},{8,9},{9,10},{10,11},{12,13},{... | collective-permute-start | bytes 36872 | tf_op jit(solution)/shard_map/ppermute | solution.py:20
  321.5 1.4 collective-permute-done.50
  324.5 5.6 %collective-permute-start.52 = (f32[4,1,32,128]{3,2,1,0:T(8,128)S(1)}, f32[4,1,32,128]{3,2,1,0:T(8,128)S(1)}, u32[]{:S(2)}, u32[]{:S(2)}) collective-permute-start(f32[4,1,32,128]{3,2,1,0:T(8,128)S(1)} %get-tuple-element.126), channel_id=1, source_target_pairs={{0,4},{4,8},{8,12},{12,16},{16,20},{20,24},{24,28},{28,32},{32,36}... | collective-permute-start | bytes 196616 | tf_op jit(solution)/shard_map/ppermute | solution.py:20
  331.0 1.9 collective-permute-start.55
  332.9 6.0 %collective-permute-start.54 = (f32[4,6,1,128]{3,2,1,0:T(1,128)S(1)}, f32[4,6,1,128]{3,2,1,0:T(1,128)S(1)}, u32[]{:S(2)}, u32[]{:S(2)}) collective-permute-start(f32[4,6,1,128]{3,2,1,0:T(1,128)S(1)} %get-tuple-element.96), channel_id=1, source_target_pairs={{0,1},{1,2},{2,3},{4,5},{5,6},{6,7},{8,9},{9,10},{10,11},{12,13},{... | collective-permute-start | bytes 36872 | tf_op jit(solution)/shard_map/ppermute | solution.py:20
  339.0 1.4 collective-permute-done.54
  342.0 5.6 %collective-permute-start.56 = (f32[4,1,32,128]{3,2,1,0:T(8,128)S(1)}, f32[4,1,32,128]{3,2,1,0:T(8,128)S(1)}, u32[]{:S(2)}, u32[]{:S(2)}) collective-permute-start(f32[4,1,32,128]{3,2,1,0:T(8,128)S(1)} %get-tuple-element.124), channel_id=1, source_target_pairs={{0,4},{4,8},{8,12},{12,16},{16,20},{20,24},{24,28},{28,32},{32,36}... | collective-permute-start | bytes 196616 | tf_op jit(solution)/shard_map/ppermute | solution.py:20
  348.5 1.9 collective-permute-start.59
  350.4 6.0 %collective-permute-start.58 = (f32[4,6,1,128]{3,2,1,0:T(1,128)S(1)}, f32[4,6,1,128]{3,2,1,0:T(1,128)S(1)}, u32[]{:S(2)}, u32[]{:S(2)}) collective-permute-start(f32[4,6,1,128]{3,2,1,0:T(1,128)S(1)} %get-tuple-element.94), channel_id=1, source_target_pairs={{0,1},{1,2},{2,3},{4,5},{5,6},{6,7},{8,9},{9,10},{10,11},{12,13},{... | collective-permute-start | bytes 36872 | tf_op jit(solution)/shard_map/ppermute | solution.py:20
  356.5 1.4 collective-permute-done.58
  359.6 5.7 %collective-permute-start.60 = (f32[8,1,32,128]{3,2,1,0:T(8,128)S(1)}, f32[8,1,32,128]{3,2,1,0:T(8,128)S(1)}, u32[]{:S(2)}, u32[]{:S(2)}) collective-permute-start(f32[8,1,32,128]{3,2,1,0:T(8,128)S(1)} %get-tuple-element.90), channel_id=1, source_target_pairs={{0,4},{4,8},{8,12},{12,16},{16,20},{20,24},{24,28},{28,32},{32,36}... | collective-permute-start | bytes 393224 | tf_op jit(solution)/shard_map/ppermute | solution.py:20
  366.4 2.1 collective-permute-start.63
  368.4 6.0 %collective-permute-start.62 = (f32[8,6,1,128]{3,2,1,0:T(1,128)S(1)}, f32[8,6,1,128]{3,2,1,0:T(1,128)S(1)}, u32[]{:S(2)}, u32[]{:S(2)}) collective-permute-start(f32[8,6,1,128]{3,2,1,0:T(1,128)S(1)} %get-tuple-element.82), channel_id=1, source_target_pairs={{0,1},{1,2},{2,3},{4,5},{5,6},{6,7},{8,9},{9,10},{10,11},{12,13},{... | collective-permute-start | bytes 73736 | tf_op jit(solution)/shard_map/ppermute | solution.py:20
  377.0 100.7 %all-reduce.21.cloned.1.call-done = f32[4,32,128]{2,1,0:T(8,128)} async-done(((f32[4,32,128]{2,1,0:T(8,128)}), f32[4,32,128]{2,1,0:T(8,128)}) %all-reduce.21.cloned.1.call-update) | async-done | bytes 65552 | tf_op jit(solution)/shard_map/psum | solution.py:99
  (204 shorter events, 55.3 us)
Async XLA Ops:
  6.5 471.2 %all-reduce.21.cloned.1.call-start = ((), (), s32[]{:S(2)}) async-start(), calls=%async_computation | async-start | bytes 131072 | tf_op jit(solution)/shard_map/psum | solution.py:99
  36.5 13.1 %collective-permute-start.1 = (f32[1,1,32,128]{2,1,3,0:T(1,128)S(1)}, f32[1,1,32,128]{2,1,3,0:T(1,128)S(1)}, u32[]{:S(2)}, u32[]{:S(2)}) collective-permute-start(f32[1,1,32,128]{2,1,3,0:T(1,128)S(1)} %get-tuple-element.153), channel_id=1, source_target_pairs={{4,0},{8,4},{12,8},{16,12},{20,16},{24,20},{28,24},{32,28},{36,32}... | collective-permute-start | bytes 49160 | tf_op jit(solution)/shard_map/ppermute | solution.py:23
  37.8 11.8 %collective-permute-start = (f32[1,1,32,128]{2,1,3,0:T(1,128)S(1)}, f32[1,1,32,128]{2,1,3,0:T(1,128)S(1)}, u32[]{:S(2)}, u32[]{:S(2)}) collective-permute-start(f32[1,1,32,128]{2,1,3,0:T(1,128)S(1)} %get-tuple-element.152), channel_id=1, source_target_pairs={{0,4},{4,8},{8,12},{12,16},{16,20},{20,24},{24,28},{28,32},{32,36}... | collective-permute-start | bytes 49160 | tf_op jit(solution)/shard_map/ppermute | solution.py:20
  40.9 41.4 %collective-permute-start.4 = (f32[4,1,32,128]{3,2,1,0:T(8,128)S(1)}, f32[4,1,32,128]{3,2,1,0:T(8,128)S(1)}, u32[]{:S(2)}, u32[]{:S(2)}) collective-permute-start(f32[4,1,32,128]{3,2,1,0:T(8,128)S(1)} %get-tuple-element.151), channel_id=1, source_target_pairs={{0,4},{4,8},{8,12},{12,16},{16,20},{20,24},{24,28},{28,32},{32,36}... | collective-permute-start | bytes 196616 | tf_op jit(solution)/shard_map/ppermute | solution.py:20
  44.8 37.5 %collective-permute-start.5 = (f32[4,1,32,128]{3,2,1,0:T(8,128)S(1)}, f32[4,1,32,128]{3,2,1,0:T(8,128)S(1)}, u32[]{:S(2)}, u32[]{:S(2)}) collective-permute-start(f32[4,1,32,128]{3,2,1,0:T(8,128)S(1)} %get-tuple-element.150), channel_id=1, source_target_pairs={{4,0},{8,4},{12,8},{16,12},{20,16},{24,20},{28,24},{32,28},{36,32}... | collective-permute-start | bytes 196616 | tf_op jit(solution)/shard_map/ppermute | solution.py:23
  50.0 29.9 %collective-permute-start.3 = (f32[1,6,1,128]{2,1,3,0:T(8,128)S(1)}, f32[1,6,1,128]{2,1,3,0:T(8,128)S(1)}, u32[]{:S(2)}, u32[]{:S(2)}) collective-permute-start(f32[1,6,1,128]{2,1,3,0:T(8,128)S(1)} %get-tuple-element.93), channel_id=1, source_target_pairs={{1,0},{2,1},{3,2},{5,4},{6,5},{7,6},{9,8},{10,9},{11,10},{13,12},{... | collective-permute-start | bytes 9224 | tf_op jit(solution)/shard_map/ppermute | solution.py:23
  55.4 24.5 %collective-permute-start.2 = (f32[1,6,1,128]{2,1,3,0:T(8,128)S(1)}, f32[1,6,1,128]{2,1,3,0:T(8,128)S(1)}, u32[]{:S(2)}, u32[]{:S(2)}) collective-permute-start(f32[1,6,1,128]{2,1,3,0:T(8,128)S(1)} %get-tuple-element.92), channel_id=1, source_target_pairs={{0,1},{1,2},{2,3},{4,5},{5,6},{6,7},{8,9},{9,10},{10,11},{12,13},{... | collective-permute-start | bytes 9224 | tf_op jit(solution)/shard_map/ppermute | solution.py:20
  82.3 11.8 %collective-permute-start.7 = (f32[4,6,1,128]{3,2,1,0:T(1,128)S(1)}, f32[4,6,1,128]{3,2,1,0:T(1,128)S(1)}, u32[]{:S(2)}, u32[]{:S(2)}) collective-permute-start(f32[4,6,1,128]{3,2,1,0:T(1,128)S(1)} %get-tuple-element.121), channel_id=1, source_target_pairs={{1,0},{2,1},{3,2},{5,4},{6,5},{7,6},{9,8},{10,9},{11,10},{13,12},{... | collective-permute-start | bytes 36872 | tf_op jit(solution)/shard_map/ppermute | solution.py:23
  84.7 9.4 %collective-permute-start.6 = (f32[4,6,1,128]{3,2,1,0:T(1,128)S(1)}, f32[4,6,1,128]{3,2,1,0:T(1,128)S(1)}, u32[]{:S(2)}, u32[]{:S(2)}) collective-permute-start(f32[4,6,1,128]{3,2,1,0:T(1,128)S(1)} %get-tuple-element.120), channel_id=1, source_target_pairs={{0,1},{1,2},{2,3},{4,5},{5,6},{6,7},{8,9},{9,10},{10,11},{12,13},{... | collective-permute-start | bytes 36872 | tf_op jit(solution)/shard_map/ppermute | solution.py:20
  95.2 4.3 collective-permute-start.9
  96.5 3.9 collective-permute-start.8
  100.5 8.0 %collective-permute-start.11 = (f32[4,6,1,128]{3,2,1,0:T(1,128)S(1)}, f32[4,6,1,128]{3,2,1,0:T(1,128)S(1)}, u32[]{:S(2)}, u32[]{:S(2)}) collective-permute-start(f32[4,6,1,128]{3,2,1,0:T(1,128)S(1)} %get-tuple-element.119), channel_id=1, source_target_pairs={{1,0},{2,1},{3,2},{5,4},{6,5},{7,6},{9,8},{10,9},{11,10},{13,12},{... | collective-permute-start | bytes 36872 | tf_op jit(solution)/shard_map/ppermute | solution.py:23
  102.4 7.4 %collective-permute-start.10 = (f32[4,6,1,128]{3,2,1,0:T(1,128)S(1)}, f32[4,6,1,128]{3,2,1,0:T(1,128)S(1)}, u32[]{:S(2)}, u32[]{:S(2)}) collective-permute-start(f32[4,6,1,128]{3,2,1,0:T(1,128)S(1)} %get-tuple-element.118), channel_id=1, source_target_pairs={{0,1},{1,2},{2,3},{4,5},{5,6},{6,7},{8,9},{9,10},{10,11},{12,13},{... | collective-permute-start | bytes 36872 | tf_op jit(solution)/shard_map/ppermute | solution.py:20
  110.1 7.1 %collective-permute-start.13 = (f32[4,1,32,128]{3,2,1,0:T(8,128)S(1)}, f32[4,1,32,128]{3,2,1,0:T(8,128)S(1)}, u32[]{:S(2)}, u32[]{:S(2)}) collective-permute-start(f32[4,1,32,128]{3,2,1,0:T(8,128)S(1)} %get-tuple-element.147), channel_id=1, source_target_pairs={{4,0},{8,4},{12,8},{16,12},{20,16},{24,20},{28,24},{32,28},{36,32}... | collective-permute-start | bytes 196616 | tf_op jit(solution)/shard_map/ppermute | solution.py:23
  111.4 6.7 %collective-permute-start.12 = (f32[4,1,32,128]{3,2,1,0:T(8,128)S(1)}, f32[4,1,32,128]{3,2,1,0:T(8,128)S(1)}, u32[]{:S(2)}, u32[]{:S(2)}) collective-permute-start(f32[4,1,32,128]{3,2,1,0:T(8,128)S(1)} %get-tuple-element.146), channel_id=1, source_target_pairs={{0,4},{4,8},{8,12},{12,16},{16,20},{20,24},{24,28},{28,32},{32,36}... | collective-permute-start | bytes 196616 | tf_op jit(solution)/shard_map/ppermute | solution.py:20
  118.2 8.0 %collective-permute-start.15 = (f32[4,6,1,128]{3,2,1,0:T(1,128)S(1)}, f32[4,6,1,128]{3,2,1,0:T(1,128)S(1)}, u32[]{:S(2)}, u32[]{:S(2)}) collective-permute-start(f32[4,6,1,128]{3,2,1,0:T(1,128)S(1)} %get-tuple-element.117), channel_id=1, source_target_pairs={{1,0},{2,1},{3,2},{5,4},{6,5},{7,6},{9,8},{10,9},{11,10},{13,12},{... | collective-permute-start | bytes 36872 | tf_op jit(solution)/shard_map/ppermute | solution.py:23
  120.1 7.4 %collective-permute-start.14 = (f32[4,6,1,128]{3,2,1,0:T(1,128)S(1)}, f32[4,6,1,128]{3,2,1,0:T(1,128)S(1)}, u32[]{:S(2)}, u32[]{:S(2)}) collective-permute-start(f32[4,6,1,128]{3,2,1,0:T(1,128)S(1)} %get-tuple-element.116), channel_id=1, source_target_pairs={{0,1},{1,2},{2,3},{4,5},{5,6},{6,7},{8,9},{9,10},{10,11},{12,13},{... | collective-permute-start | bytes 36872 | tf_op jit(solution)/shard_map/ppermute | solution.py:20
  127.8 7.3 %collective-permute-start.17 = (f32[4,1,32,128]{3,2,1,0:T(8,128)S(1)}, f32[4,1,32,128]{3,2,1,0:T(8,128)S(1)}, u32[]{:S(2)}, u32[]{:S(2)}) collective-permute-start(f32[4,1,32,128]{3,2,1,0:T(8,128)S(1)} %get-tuple-element.145), channel_id=1, source_target_pairs={{4,0},{8,4},{12,8},{16,12},{20,16},{24,20},{28,24},{32,28},{36,32}... | collective-permute-start | bytes 196616 | tf_op jit(solution)/shard_map/ppermute | solution.py:23
  129.3 6.8 %collective-permute-start.16 = (f32[4,1,32,128]{3,2,1,0:T(8,128)S(1)}, f32[4,1,32,128]{3,2,1,0:T(8,128)S(1)}, u32[]{:S(2)}, u32[]{:S(2)}) collective-permute-start(f32[4,1,32,128]{3,2,1,0:T(8,128)S(1)} %get-tuple-element.144), channel_id=1, source_target_pairs={{0,4},{4,8},{8,12},{12,16},{16,20},{20,24},{24,28},{28,32},{32,36}... | collective-permute-start | bytes 196616 | tf_op jit(solution)/shard_map/ppermute | solution.py:20
  136.1 15.5 %collective-permute-start.19 = (f32[4,6,1,128]{3,2,1,0:T(1,128)S(1)}, f32[4,6,1,128]{3,2,1,0:T(1,128)S(1)}, u32[]{:S(2)}, u32[]{:S(2)}) collective-permute-start(f32[4,6,1,128]{3,2,1,0:T(1,128)S(1)} %get-tuple-element.115), channel_id=1, source_target_pairs={{1,0},{2,1},{3,2},{5,4},{6,5},{7,6},{9,8},{10,9},{11,10},{13,12},{... | collective-permute-start | bytes 36872 | tf_op jit(solution)/shard_map/ppermute | solution.py:23
  138.0 13.6 %collective-permute-start.18 = (f32[4,6,1,128]{3,2,1,0:T(1,128)S(1)}, f32[4,6,1,128]{3,2,1,0:T(1,128)S(1)}, u32[]{:S(2)}, u32[]{:S(2)}) collective-permute-start(f32[4,6,1,128]{3,2,1,0:T(1,128)S(1)} %get-tuple-element.114), channel_id=1, source_target_pairs={{0,1},{1,2},{2,3},{4,5},{5,6},{6,7},{8,9},{9,10},{10,11},{12,13},{... | collective-permute-start | bytes 36872 | tf_op jit(solution)/shard_map/ppermute | solution.py:20
  144.7 32.1 %collective-permute-start.32 = (f32[4,1,32,128]{3,2,1,0:T(8,128)}, f32[4,1,32,128]{3,2,1,0:T(8,128)S(1)}, u32[]{:S(2)}, u32[]{:S(2)}) collective-permute-start(f32[4,1,32,128]{3,2,1,0:T(8,128)} %get-tuple-element.137), channel_id=1, source_target_pairs={{0,4},{4,8},{8,12},{12,16},{16,20},{20,24},{24,28},{28,32},{32,36}... | collective-permute-start | bytes 196616 | tf_op jit(solution)/shard_map/ppermute | solution.py:20
  150.2 43.6 %collective-permute-start.33 = (f32[4,1,32,128]{3,2,1,0:T(8,128)}, f32[4,1,32,128]{3,2,1,0:T(8,128)}, u32[]{:S(2)}, u32[]{:S(2)}) collective-permute-start(f32[4,1,32,128]{3,2,1,0:T(8,128)} %get-tuple-element.136), channel_id=1, source_target_pairs={{4,0},{8,4},{12,8},{16,12},{20,16},{24,20},{28,24},{32,28},{36,32}... | collective-permute-start | bytes 196616 | tf_op jit(solution)/shard_map/ppermute | solution.py:23
  151.9 7.7 %collective-permute-start.21 = (f32[4,1,32,128]{3,2,1,0:T(8,128)S(1)}, f32[4,1,32,128]{3,2,1,0:T(8,128)S(1)}, u32[]{:S(2)}, u32[]{:S(2)}) collective-permute-start(f32[4,1,32,128]{3,2,1,0:T(8,128)S(1)} %get-tuple-element.143), channel_id=1, source_target_pairs={{4,0},{8,4},{12,8},{16,12},{20,16},{24,20},{28,24},{32,28},{36,32}... | collective-permute-start | bytes 196616 | tf_op jit(solution)/shard_map/ppermute | solution.py:23
  153.2 6.7 %collective-permute-start.20 = (f32[4,1,32,128]{3,2,1,0:T(8,128)S(1)}, f32[4,1,32,128]{3,2,1,0:T(8,128)S(1)}, u32[]{:S(2)}, u32[]{:S(2)}) collective-permute-start(f32[4,1,32,128]{3,2,1,0:T(8,128)S(1)} %get-tuple-element.142), channel_id=1, source_target_pairs={{0,4},{4,8},{8,12},{12,16},{16,20},{20,24},{24,28},{28,32},{32,36}... | collective-permute-start | bytes 196616 | tf_op jit(solution)/shard_map/ppermute | solution.py:20
  160.5 9.8 %collective-permute-start.23 = (f32[4,6,1,128]{3,2,1,0:T(1,128)}, f32[4,6,1,128]{3,2,1,0:T(1,128)}, u32[]{:S(2)}, u32[]{:S(2)}) collective-permute-start(f32[4,6,1,128]{3,2,1,0:T(1,128)} %get-tuple-element.113), channel_id=1, source_target_pairs={{1,0},{2,1},{3,2},{5,4},{6,5},{7,6},{9,8},{10,9},{11,10},{13,12},{... | collective-permute-start | bytes 36872 | tf_op jit(solution)/shard_map/ppermute | solution.py:23
  162.4 7.9 %collective-permute-start.22 = (f32[4,6,1,128]{3,2,1,0:T(1,128)}, f32[4,6,1,128]{3,2,1,0:T(1,128)}, u32[]{:S(2)}, u32[]{:S(2)}) collective-permute-start(f32[4,6,1,128]{3,2,1,0:T(1,128)} %get-tuple-element.112), channel_id=1, source_target_pairs={{0,1},{1,2},{2,3},{4,5},{5,6},{6,7},{8,9},{9,10},{10,11},{12,13},{... | collective-permute-start | bytes 36872 | tf_op jit(solution)/shard_map/ppermute | solution.py:20
  171.3 5.5 %collective-permute-start.25 = (f32[4,1,32,128]{3,2,1,0:T(8,128)S(1)}, f32[4,1,32,128]{3,2,1,0:T(8,128)S(1)}, u32[]{:S(2)}, u32[]{:S(2)}) collective-permute-start(f32[4,1,32,128]{3,2,1,0:T(8,128)S(1)} %get-tuple-element.141), channel_id=1, source_target_pairs={{4,0},{8,4},{12,8},{16,12},{20,16},{24,20},{28,24},{32,28},{36,32}... | collective-permute-start | bytes 196616 | tf_op jit(solution)/shard_map/ppermute | solution.py:23
  172.6 5.0 %collective-permute-start.24 = (f32[4,1,32,128]{3,2,1,0:T(8,128)S(1)}, f32[4,1,32,128]{3,2,1,0:T(8,128)S(1)}, u32[]{:S(2)}, u32[]{:S(2)}) collective-permute-start(f32[4,1,32,128]{3,2,1,0:T(8,128)S(1)} %get-tuple-element.140), channel_id=1, source_target_pairs={{0,4},{4,8},{8,12},{12,16},{16,20},{20,24},{24,28},{28,32},{32,36}... | collective-permute-start | bytes 196616 | tf_op jit(solution)/shard_map/ppermute | solution.py:20
  177.7 8.0 %collective-permute-start.27 = (f32[4,6,1,128]{3,2,1,0:T(1,128)S(1)}, f32[4,6,1,128]{3,2,1,0:T(1,128)S(1)}, u32[]{:S(2)}, u32[]{:S(2)}) collective-permute-start(f32[4,6,1,128]{3,2,1,0:T(1,128)S(1)} %get-tuple-element.111), channel_id=1, source_target_pairs={{1,0},{2,1},{3,2},{5,4},{6,5},{7,6},{9,8},{10,9},{11,10},{13,12},{... | collective-permute-start | bytes 36872 | tf_op jit(solution)/shard_map/ppermute | solution.py:23
  179.6 7.4 %collective-permute-start.26 = (f32[4,6,1,128]{3,2,1,0:T(1,128)S(1)}, f32[4,6,1,128]{3,2,1,0:T(1,128)S(1)}, u32[]{:S(2)}, u32[]{:S(2)}) collective-permute-start(f32[4,6,1,128]{3,2,1,0:T(1,128)S(1)} %get-tuple-element.110), channel_id=1, source_target_pairs={{0,1},{1,2},{2,3},{4,5},{5,6},{6,7},{8,9},{9,10},{10,11},{12,13},{... | collective-permute-start | bytes 36872 | tf_op jit(solution)/shard_map/ppermute | solution.py:20
  187.3 7.3 %collective-permute-start.29 = (f32[4,1,32,128]{3,2,1,0:T(8,128)S(1)}, f32[4,1,32,128]{3,2,1,0:T(8,128)S(1)}, u32[]{:S(2)}, u32[]{:S(2)}) collective-permute-start(f32[4,1,32,128]{3,2,1,0:T(8,128)S(1)} %get-tuple-element.139), channel_id=1, source_target_pairs={{4,0},{8,4},{12,8},{16,12},{20,16},{24,20},{28,24},{32,28},{36,32}... | collective-permute-start | bytes 196616 | tf_op jit(solution)/shard_map/ppermute | solution.py:23
  188.6 6.0 %collective-permute-start.28 = (f32[4,1,32,128]{3,2,1,0:T(8,128)S(1)}, f32[4,1,32,128]{3,2,1,0:T(8,128)S(1)}, u32[]{:S(2)}, u32[]{:S(2)}) collective-permute-start(f32[4,1,32,128]{3,2,1,0:T(8,128)S(1)} %get-tuple-element.138), channel_id=1, source_target_pairs={{0,4},{4,8},{8,12},{12,16},{16,20},{20,24},{24,28},{28,32},{32,36}... | collective-permute-start | bytes 196616 | tf_op jit(solution)/shard_map/ppermute | solution.py:20
  194.7 16.0 %collective-permute-start.31 = (f32[4,6,1,128]{3,2,1,0:T(1,128)S(1)}, f32[4,6,1,128]{3,2,1,0:T(1,128)S(1)}, u32[]{:S(2)}, u32[]{:S(2)}) collective-permute-start(f32[4,6,1,128]{3,2,1,0:T(1,128)S(1)} %get-tuple-element.109), channel_id=1, source_target_pairs={{1,0},{2,1},{3,2},{5,4},{6,5},{7,6},{9,8},{10,9},{11,10},{13,12},{... | collective-permute-start | bytes 36872 | tf_op jit(solution)/shard_map/ppermute | solution.py:23
  196.6 14.0 %collective-permute-start.30 = (f32[4,6,1,128]{3,2,1,0:T(1,128)S(1)}, f32[4,6,1,128]{3,2,1,0:T(1,128)S(1)}, u32[]{:S(2)}, u32[]{:S(2)}) collective-permute-start(f32[4,6,1,128]{3,2,1,0:T(1,128)S(1)} %get-tuple-element.108), channel_id=1, source_target_pairs={{0,1},{1,2},{2,3},{4,5},{5,6},{6,7},{8,9},{9,10},{10,11},{12,13},{... | collective-permute-start | bytes 36872 | tf_op jit(solution)/shard_map/ppermute | solution.py:20
  202.7 53.5 %collective-permute-start.35 = (f32[4,6,1,128]{3,2,1,0:T(1,128)S(1)}, f32[4,6,1,128]{3,2,1,0:T(1,128)S(1)}, u32[]{:S(2)}, u32[]{:S(2)}) collective-permute-start(f32[4,6,1,128]{3,2,1,0:T(1,128)S(1)} %get-tuple-element.107), channel_id=1, source_target_pairs={{1,0},{2,1},{3,2},{5,4},{6,5},{7,6},{9,8},{10,9},{11,10},{13,12},{... | collective-permute-start | bytes 36872 | tf_op jit(solution)/shard_map/ppermute | solution.py:23
  204.6 51.5 %collective-permute-start.34 = (f32[4,6,1,128]{3,2,1,0:T(1,128)S(1)}, f32[4,6,1,128]{3,2,1,0:T(1,128)S(1)}, u32[]{:S(2)}, u32[]{:S(2)}) collective-permute-start(f32[4,6,1,128]{3,2,1,0:T(1,128)S(1)} %get-tuple-element.106), channel_id=1, source_target_pairs={{0,1},{1,2},{2,3},{4,5},{5,6},{6,7},{8,9},{9,10},{10,11},{12,13},{... | collective-permute-start | bytes 36872 | tf_op jit(solution)/shard_map/ppermute | solution.py:20
  257.3 4.3 collective-permute-start.37
  258.6 3.9 collective-permute-start.36
  262.6 8.0 %collective-permute-start.39 = (f32[4,6,1,128]{3,2,1,0:T(1,128)S(1)}, f32[4,6,1,128]{3,2,1,0:T(1,128)S(1)}, u32[]{:S(2)}, u32[]{:S(2)}) collective-permute-start(f32[4,6,1,128]{3,2,1,0:T(1,128)S(1)} %get-tuple-element.105), channel_id=1, source_target_pairs={{1,0},{2,1},{3,2},{5,4},{6,5},{7,6},{9,8},{10,9},{11,10},{13,12},{... | collective-permute-start | bytes 36872 | tf_op jit(solution)/shard_map/ppermute | solution.py:23
  266.9 6.5 %collective-permute-start.38 = (f32[4,6,1,128]{3,2,1,0:T(1,128)S(1)}, f32[4,6,1,128]{3,2,1,0:T(1,128)S(1)}, u32[]{:S(2)}, u32[]{:S(2)}) collective-permute-start(f32[4,6,1,128]{3,2,1,0:T(1,128)S(1)} %get-tuple-element.104), channel_id=1, source_target_pairs={{0,1},{1,2},{2,3},{4,5},{5,6},{6,7},{8,9},{9,10},{10,11},{12,13},{... | collective-permute-start | bytes 36872 | tf_op jit(solution)/shard_map/ppermute | solution.py:20
  273.7 4.3 collective-permute-start.41
  279.0 8.0 %collective-permute-start.43 = (f32[4,6,1,128]{3,2,1,0:T(1,128)S(1)}, f32[4,6,1,128]{3,2,1,0:T(1,128)S(1)}, u32[]{:S(2)}, u32[]{:S(2)}) collective-permute-start(f32[4,6,1,128]{3,2,1,0:T(1,128)S(1)} %get-tuple-element.103), channel_id=1, source_target_pairs={{1,0},{2,1},{3,2},{5,4},{6,5},{7,6},{9,8},{10,9},{11,10},{13,12},{... | collective-permute-start | bytes 36872 | tf_op jit(solution)/shard_map/ppermute | solution.py:23
  280.9 7.4 %collective-permute-start.42 = (f32[4,6,1,128]{3,2,1,0:T(1,128)S(1)}, f32[4,6,1,128]{3,2,1,0:T(1,128)S(1)}, u32[]{:S(2)}, u32[]{:S(2)}) collective-permute-start(f32[4,6,1,128]{3,2,1,0:T(1,128)S(1)} %get-tuple-element.102), channel_id=1, source_target_pairs={{0,1},{1,2},{2,3},{4,5},{5,6},{6,7},{8,9},{9,10},{10,11},{12,13},{... | collective-permute-start | bytes 36872 | tf_op jit(solution)/shard_map/ppermute | solution.py:20
  288.6 6.3 %collective-permute-start.45 = (f32[4,1,32,128]{3,2,1,0:T(8,128)S(1)}, f32[4,1,32,128]{3,2,1,0:T(8,128)S(1)}, u32[]{:S(2)}, u32[]{:S(2)}) collective-permute-start(f32[4,1,32,128]{3,2,1,0:T(8,128)S(1)} %get-tuple-element.131), channel_id=1, source_target_pairs={{4,0},{8,4},{12,8},{16,12},{20,16},{24,20},{28,24},{32,28},{36,32}... | collective-permute-start | bytes 196616 | tf_op jit(solution)/shard_map/ppermute | solution.py:23
  289.9 5.7 %collective-permute-start.44 = (f32[4,1,32,128]{3,2,1,0:T(8,128)S(1)}, f32[4,1,32,128]{3,2,1,0:T(8,128)S(1)}, u32[]{:S(2)}, u32[]{:S(2)}) collective-permute-start(f32[4,1,32,128]{3,2,1,0:T(8,128)S(1)} %get-tuple-element.130), channel_id=1, source_target_pairs={{0,4},{4,8},{8,12},{12,16},{16,20},{20,24},{24,28},{28,32},{32,36}... | collective-permute-start | bytes 196616 | tf_op jit(solution)/shard_map/ppermute | solution.py:20
  295.7 8.0 %collective-permute-start.47 = (f32[4,6,1,128]{3,2,1,0:T(1,128)S(1)}, f32[4,6,1,128]{3,2,1,0:T(1,128)S(1)}, u32[]{:S(2)}, u32[]{:S(2)}) collective-permute-start(f32[4,6,1,128]{3,2,1,0:T(1,128)S(1)} %get-tuple-element.101), channel_id=1, source_target_pairs={{1,0},{2,1},{3,2},{5,4},{6,5},{7,6},{9,8},{10,9},{11,10},{13,12},{... | collective-permute-start | bytes 36872 | tf_op jit(solution)/shard_map/ppermute | solution.py:23
  297.6 7.4 %collective-permute-start.46 = (f32[4,6,1,128]{3,2,1,0:T(1,128)S(1)}, f32[4,6,1,128]{3,2,1,0:T(1,128)S(1)}, u32[]{:S(2)}, u32[]{:S(2)}) collective-permute-start(f32[4,6,1,128]{3,2,1,0:T(1,128)S(1)} %get-tuple-element.100), channel_id=1, source_target_pairs={{0,1},{1,2},{2,3},{4,5},{5,6},{6,7},{8,9},{9,10},{10,11},{12,13},{... | collective-permute-start | bytes 36872 | tf_op jit(solution)/shard_map/ppermute | solution.py:20
  305.3 7.3 %collective-permute-start.49 = (f32[4,1,32,128]{3,2,1,0:T(8,128)S(1)}, f32[4,1,32,128]{3,2,1,0:T(8,128)S(1)}, u32[]{:S(2)}, u32[]{:S(2)}) collective-permute-start(f32[4,1,32,128]{3,2,1,0:T(8,128)S(1)} %get-tuple-element.129), channel_id=1, source_target_pairs={{4,0},{8,4},{12,8},{16,12},{20,16},{24,20},{28,24},{32,28},{36,32}... | collective-permute-start | bytes 196616 | tf_op jit(solution)/shard_map/ppermute | solution.py:23
  306.6 6.9 %collective-permute-start.48 = (f32[4,1,32,128]{3,2,1,0:T(8,128)S(1)}, f32[4,1,32,128]{3,2,1,0:T(8,128)S(1)}, u32[]{:S(2)}, u32[]{:S(2)}) collective-permute-start(f32[4,1,32,128]{3,2,1,0:T(8,128)S(1)} %get-tuple-element.128), channel_id=1, source_target_pairs={{0,4},{4,8},{8,12},{12,16},{16,20},{20,24},{24,28},{28,32},{32,36}... | collective-permute-start | bytes 196616 | tf_op jit(solution)/shard_map/ppermute | solution.py:20
  313.5 8.0 %collective-permute-start.51 = (f32[4,6,1,128]{3,2,1,0:T(1,128)S(1)}, f32[4,6,1,128]{3,2,1,0:T(1,128)S(1)}, u32[]{:S(2)}, u32[]{:S(2)}) collective-permute-start(f32[4,6,1,128]{3,2,1,0:T(1,128)S(1)} %get-tuple-element.99), channel_id=1, source_target_pairs={{1,0},{2,1},{3,2},{5,4},{6,5},{7,6},{9,8},{10,9},{11,10},{13,12},{... | collective-permute-start | bytes 36872 | tf_op jit(solution)/shard_map/ppermute | solution.py:23
  315.5 7.4 %collective-permute-start.50 = (f32[4,6,1,128]{3,2,1,0:T(1,128)S(1)}, f32[4,6,1,128]{3,2,1,0:T(1,128)S(1)}, u32[]{:S(2)}, u32[]{:S(2)}) collective-permute-start(f32[4,6,1,128]{3,2,1,0:T(1,128)S(1)} %get-tuple-element.98), channel_id=1, source_target_pairs={{0,1},{1,2},{2,3},{4,5},{5,6},{6,7},{8,9},{9,10},{10,11},{12,13},{... | collective-permute-start | bytes 36872 | tf_op jit(solution)/shard_map/ppermute | solution.py:20
  323.2 6.9 %collective-permute-start.53 = (f32[4,1,32,128]{3,2,1,0:T(8,128)S(1)}, f32[4,1,32,128]{3,2,1,0:T(8,128)S(1)}, u32[]{:S(2)}, u32[]{:S(2)}) collective-permute-start(f32[4,1,32,128]{3,2,1,0:T(8,128)S(1)} %get-tuple-element.127), channel_id=1, source_target_pairs={{4,0},{8,4},{12,8},{16,12},{20,16},{24,20},{28,24},{32,28},{36,32}... | collective-permute-start | bytes 196616 | tf_op jit(solution)/shard_map/ppermute | solution.py:23
  324.5 6.5 %collective-permute-start.52 = (f32[4,1,32,128]{3,2,1,0:T(8,128)S(1)}, f32[4,1,32,128]{3,2,1,0:T(8,128)S(1)}, u32[]{:S(2)}, u32[]{:S(2)}) collective-permute-start(f32[4,1,32,128]{3,2,1,0:T(8,128)S(1)} %get-tuple-element.126), channel_id=1, source_target_pairs={{0,4},{4,8},{8,12},{12,16},{16,20},{20,24},{24,28},{28,32},{32,36}... | collective-permute-start | bytes 196616 | tf_op jit(solution)/shard_map/ppermute | solution.py:20
  331.0 8.0 %collective-permute-start.55 = (f32[4,6,1,128]{3,2,1,0:T(1,128)S(1)}, f32[4,6,1,128]{3,2,1,0:T(1,128)S(1)}, u32[]{:S(2)}, u32[]{:S(2)}) collective-permute-start(f32[4,6,1,128]{3,2,1,0:T(1,128)S(1)} %get-tuple-element.97), channel_id=1, source_target_pairs={{1,0},{2,1},{3,2},{5,4},{6,5},{7,6},{9,8},{10,9},{11,10},{13,12},{... | collective-permute-start | bytes 36872 | tf_op jit(solution)/shard_map/ppermute | solution.py:23
  332.9 7.4 %collective-permute-start.54 = (f32[4,6,1,128]{3,2,1,0:T(1,128)S(1)}, f32[4,6,1,128]{3,2,1,0:T(1,128)S(1)}, u32[]{:S(2)}, u32[]{:S(2)}) collective-permute-start(f32[4,6,1,128]{3,2,1,0:T(1,128)S(1)} %get-tuple-element.96), channel_id=1, source_target_pairs={{0,1},{1,2},{2,3},{4,5},{5,6},{6,7},{8,9},{9,10},{10,11},{12,13},{... | collective-permute-start | bytes 36872 | tf_op jit(solution)/shard_map/ppermute | solution.py:20
  340.7 6.9 %collective-permute-start.57 = (f32[4,1,32,128]{3,2,1,0:T(8,128)S(1)}, f32[4,1,32,128]{3,2,1,0:T(8,128)S(1)}, u32[]{:S(2)}, u32[]{:S(2)}) collective-permute-start(f32[4,1,32,128]{3,2,1,0:T(8,128)S(1)} %get-tuple-element.125), channel_id=1, source_target_pairs={{4,0},{8,4},{12,8},{16,12},{20,16},{24,20},{28,24},{32,28},{36,32}... | collective-permute-start | bytes 196616 | tf_op jit(solution)/shard_map/ppermute | solution.py:23
  342.0 6.5 %collective-permute-start.56 = (f32[4,1,32,128]{3,2,1,0:T(8,128)S(1)}, f32[4,1,32,128]{3,2,1,0:T(8,128)S(1)}, u32[]{:S(2)}, u32[]{:S(2)}) collective-permute-start(f32[4,1,32,128]{3,2,1,0:T(8,128)S(1)} %get-tuple-element.124), channel_id=1, source_target_pairs={{0,4},{4,8},{8,12},{12,16},{16,20},{20,24},{24,28},{28,32},{32,36}... | collective-permute-start | bytes 196616 | tf_op jit(solution)/shard_map/ppermute | solution.py:20
  348.5 8.0 %collective-permute-start.59 = (f32[4,6,1,128]{3,2,1,0:T(1,128)S(1)}, f32[4,6,1,128]{3,2,1,0:T(1,128)S(1)}, u32[]{:S(2)}, u32[]{:S(2)}) collective-permute-start(f32[4,6,1,128]{3,2,1,0:T(1,128)S(1)} %get-tuple-element.95), channel_id=1, source_target_pairs={{1,0},{2,1},{3,2},{5,4},{6,5},{7,6},{9,8},{10,9},{11,10},{13,12},{... | collective-permute-start | bytes 36872 | tf_op jit(solution)/shard_map/ppermute | solution.py:23
  350.4 7.4 %collective-permute-start.58 = (f32[4,6,1,128]{3,2,1,0:T(1,128)S(1)}, f32[4,6,1,128]{3,2,1,0:T(1,128)S(1)}, u32[]{:S(2)}, u32[]{:S(2)}) collective-permute-start(f32[4,6,1,128]{3,2,1,0:T(1,128)S(1)} %get-tuple-element.94), channel_id=1, source_target_pairs={{0,1},{1,2},{2,3},{4,5},{5,6},{6,7},{8,9},{9,10},{10,11},{12,13},{... | collective-permute-start | bytes 36872 | tf_op jit(solution)/shard_map/ppermute | solution.py:20
  358.3 7.1 %collective-permute-start.61 = (f32[8,1,32,128]{3,2,1,0:T(8,128)S(1)}, f32[8,1,32,128]{3,2,1,0:T(8,128)S(1)}, u32[]{:S(2)}, u32[]{:S(2)}) collective-permute-start(f32[8,1,32,128]{3,2,1,0:T(8,128)S(1)} %get-tuple-element.91), channel_id=1, source_target_pairs={{4,0},{8,4},{12,8},{16,12},{20,16},{24,20},{28,24},{32,28},{36,32}... | collective-permute-start | bytes 393224 | tf_op jit(solution)/shard_map/ppermute | solution.py:23
  359.6 6.7 %collective-permute-start.60 = (f32[8,1,32,128]{3,2,1,0:T(8,128)S(1)}, f32[8,1,32,128]{3,2,1,0:T(8,128)S(1)}, u32[]{:S(2)}, u32[]{:S(2)}) collective-permute-start(f32[8,1,32,128]{3,2,1,0:T(8,128)S(1)} %get-tuple-element.90), channel_id=1, source_target_pairs={{0,4},{4,8},{8,12},{12,16},{16,20},{20,24},{24,28},{28,32},{32,36}... | collective-permute-start | bytes 393224 | tf_op jit(solution)/shard_map/ppermute | solution.py:20
  366.4 8.8 %collective-permute-start.63 = (f32[8,6,1,128]{3,2,1,0:T(1,128)S(1)}, f32[8,6,1,128]{3,2,1,0:T(1,128)S(1)}, u32[]{:S(2)}, u32[]{:S(2)}) collective-permute-start(f32[8,6,1,128]{3,2,1,0:T(1,128)S(1)} %get-tuple-element.83), channel_id=1, source_target_pairs={{1,0},{2,1},{3,2},{5,4},{6,5},{7,6},{9,8},{10,9},{11,10},{13,12},{... | collective-permute-start | bytes 73736 | tf_op jit(solution)/shard_map/ppermute | solution.py:23
  368.4 7.5 %collective-permute-start.62 = (f32[8,6,1,128]{3,2,1,0:T(1,128)S(1)}, f32[8,6,1,128]{3,2,1,0:T(1,128)S(1)}, u32[]{:S(2)}, u32[]{:S(2)}) collective-permute-start(f32[8,6,1,128]{3,2,1,0:T(1,128)S(1)} %get-tuple-element.82), channel_id=1, source_target_pairs={{0,1},{1,2},{2,3},{4,5},{5,6},{6,7},{8,9},{9,10},{10,11},{12,13},{... | collective-permute-start | bytes 73736 | tf_op jit(solution)/shard_map/ppermute | solution.py:20
  (22 other events, 410.6 us)
Sparse Core Ops, SparseCore 0:
  377.1 100.5 all-reduce.20
